TPU v7x, 128 devices: a whole 4x4x4 slice. The times are simulated.
128 devices in a mesh: row: 8 (over y, core), col: 16 (over x, z).
Axes of the slice: x: 4, y: 4, z: 4, core: 2. Of those that a mesh axis runs over, the one named last changes fastest.
Arguments:
- table: float32 [512, 524288], P('col', 'row'), may hold values from -6 to 6
- accum: float32 [524288], P('row'), may hold values from 0.05 to 1
- grad_pooled: float32 [512, 16384], P('col', 'row')
- bag_of: int32 [8, 32768], P('row'), may hold values from 0 to 2047, never falling along the last dimension, each value on 1 to 64 neighbouring positions
- slots: int32 [8, 32768], P('row'), may hold values from 0 to 16383
- dirty_rows: int32 [8, 16384], P('row'), may hold values from 0 to 65535, as said below
- owner: int32 [131072, 1], P('row'), may hold values from 0 to 7; in each aligned block of 1024 rows (0 to 1023, 1024 to 2047, ...) at most 256 rows name the same one
Outputs:
- owned_rows: float32 [512, 262144], P(None, ('row', 'col'))
- accum_dirty: float32 [131072], P(('row', 'col'))
Inputs may be any that keep to these rules, and one draw needn't show every extreme that they name: `dirty_rows`: within one row shard the slots name distinct cached rows. Within each aligned block of 1024 slots no owner is named more than 256 times. `bag_of`: never falling along a shard's entries; every bag has at least one entry.
All inputs are finite; a program needn't handle non-finite values.
Results may differ from a plain program's by a relative error of at most 0.0003.
Values sent between devices are 32-bit elements; how exact they have to be, the bound alone decides.
No kernel may reach another device: no remote copies, remote signals or barrier semaphores. Data moves between devices by JAX's collectives and lax.ppermute only.
A program may use at most 192 MiB of HBM per device.

v0:
```python
import jax
import jax.numpy as jnp
from jax import lax
from jax.sharding import PartitionSpec as P

BLOCK = 128


learn_rate = 0.3
epsilon = 1e-08


def place_counts(owner_blocks, owner_count):
    length = owner_blocks.shape[-1]
    onehot = (owner_blocks[..., None] == jnp.arange(owner_count, dtype=jnp.int32)).astype(
        jnp.bfloat16
    )
    steps_idx = jnp.arange(length, dtype=jnp.int32)
    lower = (steps_idx[:, None] > steps_idx[None, :]).astype(jnp.bfloat16)
    earlier = jnp.einsum("kl,blo->bko", lower, onehot, preferred_element_type=jnp.float32)
    return jnp.sum(earlier * onehot.astype(jnp.float32), axis=-1).astype(jnp.int32)


def spread_bags(grad_pooled, bag_row):
    entries = bag_row.shape[0]
    bag_total = grad_pooled.shape[1]
    blk_len = min(512, entries)
    window = min(blk_len, bag_total)
    block_total = entries // blk_len
    groups = min(8, block_total)
    per_group = block_total // groups
    ids = bag_row.reshape(groups, per_group, blk_len)
    window_idx = jnp.arange(window, dtype=jnp.int32)

    def one_block(block_ids):
        start = jnp.minimum(block_ids[0], bag_total - window)
        piece = lax.dynamic_slice_in_dim(grad_pooled, start, window, 1)
        picker = (block_ids[None, :] - start == window_idx[:, None]).astype(jnp.float32)
        return jnp.dot(
            piece, picker, precision=lax.Precision.HIGHEST, preferred_element_type=jnp.float32
        )

    spread = lax.map(lambda group_ids: jax.vmap(one_block)(group_ids), ids)
    spread = jnp.transpose(spread, (2, 0, 1, 3))
    return spread.reshape(grad_pooled.shape[0], entries)


def place_columns(values, targets, total):
    picker = (targets[:, None] == jnp.arange(total, dtype=jnp.int32)[None, :]).astype(jnp.float32)
    return jnp.dot(
        values, picker, precision=lax.Precision.HIGHEST, preferred_element_type=jnp.float32
    )


def local(table, accum, grad_pooled, bag_of, slots, dirty_rows, owner):
    width_slice = table.shape[0]
    col_count = lax.axis_size("col")
    row_count = lax.axis_size("row")
    full_width = width_slice * col_count
    dirty_local = dirty_rows[0]
    dirty_count = dirty_local.shape[0]
    forward = dirty_count // col_count
    capacity = BLOCK * ((forward * 3 // 2 // row_count + BLOCK - 1) // BLOCK)
    entry_grad = spread_bags(grad_pooled, bag_of[0])
    row_grads = jnp.zeros((width_slice, dirty_count), jnp.float32).at[:, slots[0]].add(entry_grad)
    old_rows = jnp.take(table, dirty_local, axis=1)
    accum_old = accum[dirty_local]
    norm_total = lax.psum(jnp.sum(row_grads * row_grads, axis=0), "col")
    accum_new = accum_old + norm_total / full_width
    updated = old_rows - learn_rate * row_grads / (jnp.sqrt(accum_new) + epsilon)
    col_index = lax.axis_index("col")
    accum_dirty = lax.dynamic_slice_in_dim(accum_new, col_index * forward, forward)
    owners = owner[:, 0]
    slot_total = row_count * capacity
    blocks = owners.reshape(col_count, forward)
    places = place_counts(blocks, row_count)
    local_target = blocks * capacity + places
    value_blocks = jnp.transpose(updated.reshape(width_slice, col_count, forward), (1, 0, 2))

    def place_block(pair):
        return place_columns(pair[0], pair[1], slot_total)

    placed = lax.map(place_block, (value_blocks, local_target))
    placed = placed.reshape(col_count, width_slice, row_count, capacity)
    buffer = jnp.transpose(placed, (1, 2, 0, 3)).reshape(
        width_slice, row_count * col_count * capacity
    )
    received = lax.all_to_all(buffer, ("row", "col"), split_axis=1, concat_axis=0, tiled=True)
    received = received.reshape(row_count, full_width, capacity)
    owned_rows = jnp.transpose(received, (1, 0, 2)).reshape(full_width, row_count * capacity)
    return (owned_rows, accum_dirty)


def solution(mesh):
    return jax.shard_map(
        local,
        mesh=mesh,
        in_specs=(
            P("col", "row"),
            P("row"),
            P("col", "row"),
            P("row", None),
            P("row", None),
            P("row", None),
            P("row", None),
        ),
        out_specs=(P(None, ("row", "col")), P(("row", "col"))),
        check_vma=False,
    )
```

profile of v0, /device:TPU:7, one launch (start us, length us, event | category | flops | bytes accessed | tf_op | source)
XLA Modules:
  0.0 734.2 jit_solution(4745809433638361409)
XLA Ops:
  10.6 182.0 %while.26 = (s32[]{:T(128)}, f32[8,8,32,512]{3,2,1,0:T(8,128)}, s32[8,8,512]{2,1,0:T(8,128)S(1)}, f32[32,2048]{1,0:T(8,128)}, s32[]{:T(128)}, /*index=5*/s32[]{:T(128)}, s32[]{:T(128)}) while((s32[]{:T(128)}, f32[8,8,32,512]{3,2,1,0:T(8,128)}, s32[8,8,512]{2,1,0:T(8,128)S(1)}, f32[32,2048]{1,0:T(8,128)}, s32[]{:T(128)}, ...), condition=%wide.region_1.2_spmd.clone, body=%wide.region_0.1_spmd.clone.sunk | while | flops 807407680 | bytes 1327578 | solution.py:43
  10.8 18.7 %while.27 = (s32[]{:T(128)}, f32[32,2048]{1,0:T(8,128)}, s32[8,2]{0,1:T(2,128)S(1)}, f32[8,32,512]{2,1,0:T(8,128)S(1)}, s32[]{:T(128)}) while((s32[]{:T(128)}, f32[32,2048]{1,0:T(8,128)}, s32[8,2]{0,1:T(2,128)S(1)}, f32[8,32,512]{2,1,0:T(8,128)S(1)}, s32[]{:T(128)}) %tuple.63), condition=%wide.while_cond, body=%wide.while_body.sunk | while | flops 2 | bytes 131177 | solution.py:37
  33.6 18.7 %while.27 = (s32[]{:T(128)}, f32[32,2048]{1,0:T(8,128)}, s32[8,2]{0,1:T(2,128)S(1)}, f32[8,32,512]{2,1,0:T(8,128)S(1)}, s32[]{:T(128)}) while((s32[]{:T(128)}, f32[32,2048]{1,0:T(8,128)}, s32[8,2]{0,1:T(2,128)S(1)}, f32[8,32,512]{2,1,0:T(8,128)S(1)}, s32[]{:T(128)}) %tuple.63), condition=%wide.while_cond, body=%wide.while_body.sunk | while | flops 2 | bytes 131177 | solution.py:37
  56.5 18.7 %while.27 = (s32[]{:T(128)}, f32[32,2048]{1,0:T(8,128)}, s32[8,2]{0,1:T(2,128)S(1)}, f32[8,32,512]{2,1,0:T(8,128)S(1)}, s32[]{:T(128)}) while((s32[]{:T(128)}, f32[32,2048]{1,0:T(8,128)}, s32[8,2]{0,1:T(2,128)S(1)}, f32[8,32,512]{2,1,0:T(8,128)S(1)}, s32[]{:T(128)}) %tuple.63), condition=%wide.while_cond, body=%wide.while_body.sunk | while | flops 2 | bytes 131177 | solution.py:37
  79.3 18.7 %while.27 = (s32[]{:T(128)}, f32[32,2048]{1,0:T(8,128)}, s32[8,2]{0,1:T(2,128)S(1)}, f32[8,32,512]{2,1,0:T(8,128)S(1)}, s32[]{:T(128)}) while((s32[]{:T(128)}, f32[32,2048]{1,0:T(8,128)}, s32[8,2]{0,1:T(2,128)S(1)}, f32[8,32,512]{2,1,0:T(8,128)S(1)}, s32[]{:T(128)}) %tuple.63), condition=%wide.while_cond, body=%wide.while_body.sunk | while | flops 2 | bytes 131177 | solution.py:37
  102.2 18.7 %while.27 = (s32[]{:T(128)}, f32[32,2048]{1,0:T(8,128)}, s32[8,2]{0,1:T(2,128)S(1)}, f32[8,32,512]{2,1,0:T(8,128)S(1)}, s32[]{:T(128)}) while((s32[]{:T(128)}, f32[32,2048]{1,0:T(8,128)}, s32[8,2]{0,1:T(2,128)S(1)}, f32[8,32,512]{2,1,0:T(8,128)S(1)}, s32[]{:T(128)}) %tuple.63), condition=%wide.while_cond, body=%wide.while_body.sunk | while | flops 2 | bytes 131177 | solution.py:37
  125.0 18.7 %while.27 = (s32[]{:T(128)}, f32[32,2048]{1,0:T(8,128)}, s32[8,2]{0,1:T(2,128)S(1)}, f32[8,32,512]{2,1,0:T(8,128)S(1)}, s32[]{:T(128)}) while((s32[]{:T(128)}, f32[32,2048]{1,0:T(8,128)}, s32[8,2]{0,1:T(2,128)S(1)}, f32[8,32,512]{2,1,0:T(8,128)S(1)}, s32[]{:T(128)}) %tuple.63), condition=%wide.while_cond, body=%wide.while_body.sunk | while | flops 2 | bytes 131177 | solution.py:37
  147.8 18.3 %while.27 = (s32[]{:T(128)}, f32[32,2048]{1,0:T(8,128)}, s32[8,2]{0,1:T(2,128)S(1)}, f32[8,32,512]{2,1,0:T(8,128)S(1)}, s32[]{:T(128)}) while((s32[]{:T(128)}, f32[32,2048]{1,0:T(8,128)}, s32[8,2]{0,1:T(2,128)S(1)}, f32[8,32,512]{2,1,0:T(8,128)S(1)}, s32[]{:T(128)}) %tuple.63), condition=%wide.while_cond, body=%wide.while_body.sunk | while | flops 2 | bytes 131177 | solution.py:37
  170.3 18.3 %while.27 = (s32[]{:T(128)}, f32[32,2048]{1,0:T(8,128)}, s32[8,2]{0,1:T(2,128)S(1)}, f32[8,32,512]{2,1,0:T(8,128)S(1)}, s32[]{:T(128)}) while((s32[]{:T(128)}, f32[32,2048]{1,0:T(8,128)}, s32[8,2]{0,1:T(2,128)S(1)}, f32[8,32,512]{2,1,0:T(8,128)S(1)}, s32[]{:T(128)}) %tuple.63), condition=%wide.while_cond, body=%wide.while_body.sunk | while | flops 2 | bytes 131177 | solution.py:37
  192.6 4.7 copy.40
  197.3 10.4 %copy.33 = f32[32768,32]{1,0:T(8,128)} copy(f32[32768,32]{0,1:T(8,128)} %bitcast.92) | data formatting | bytes 8388608 | tf_op jit(solution)/shard_map/reshape | solution.py:45
  207.7 177.9 %scatter_custom_fusion = f32[32,16384]{0,1:T(8,128)} fusion(s32[32768]{0:T(1024)S(1)} %bitcast.101, f32[32768,32]{1,0:T(8,128)} %copy.33, f32[]{:T(128)} %constant.21.clone.1), kind=kCustom, calls=%fused_computation.29 | custom fusion | flops 1048576 | bytes 2097664 | tf_op jit(solution)/shard_map/scatter-add | solution.py:65
  385.6 5.3 multiply_reduce_fusion
  392.5 18.6 %copy.30 = f32[32,65536]{0,1:T(8,128)} copy(f32[32,65536]{1,0:T(8,128)} %param.11) | data formatting | bytes 16777216 | tf_op args[0]
  411.1 64.9 %gather_fusion = f32[16384,32]{1,0:T(8,128)} fusion(f32[32,65536]{0,1:T(8,128)} %copy.30, s32[16384]{0:T(1024)S(1)} %broadcast_clamp_fusion), kind=kCustom, calls=%fused_computation | custom fusion | bytes 4259840 | tf_op jit(solution)/shard_map/jit(_take)/gather | solution.py:66
  476.0 90.5 %gather_fusion.1 = f32[16384]{0:T(1024)S(1)} fusion(f32[65536]{0:T(1024)S(1)} %copy-done, s32[16384]{0:T(1024)S(1)} %broadcast_clamp_fusion), kind=kCustom, calls=%fused_computation.1 | custom fusion | bytes 196608 | tf_op jit(solution)/shard_map/gather | solution.py:67
  567.5 9.5 %bitcast_subtract_fusion = f32[32,16384]{0,1:T(8,128)} fusion(f32[16384,32]{1,0:T(8,128)} %gather_fusion, f32[32,16384]{0,1:T(8,128)} %scatter_custom_fusion, f32[16384]{0:T(1024)S(1)} %get-tuple-element.112, pred[16384]{0:T(1024)(128)(4,1)S(1)} %compare_and_fusion), kind=kLoop, calls=%fused_computation.25 | loop fusion | flops 2097152 | bytes 6373376 | tf_op jit(solution)/shard_map/sub | solution.py:70
  577.0 5.1 copy.34
  582.1 61.6 %while.24 = (s32[]{:T(128)}, f32[16,32,2048]{2,1,0:T(8,128)}, f32[16,32,1024]{2,1,0:T(8,128)S(1)}, s32[16,1024]{1,0:T(8,128)S(1)}, s32[]{:T(128)}) while((s32[]{:T(128)}, f32[16,32,2048]{2,1,0:T(8,128)}, f32[16,32,1024]{2,1,0:T(8,128)S(1)}, s32[16,1024]{1,0:T(8,128)S(1)}, s32[]{:T(128)}) %tuple.74), condition=%wide.region_7.8_spmd, body=%wide.region_6.7_spmd.sunk | while | flops 807403520 | bytes 406601 | solution.py:83
  650.7 4.4 copy.36
  655.1 11.3 %all-to-all-start = ((f32[32,128,256]{2,0,1:T(8,128)}), f32[32,128,256]{2,0,1:T(8,128)}, u32[]{:S(2)}, u32[]{:S(2)}) async-start(f32[32,128,256]{2,0,1:T(8,128)} %copy.36), calls=%async_computation | async-start | bytes 8388608 | tf_op jit(solution)/shard_map/all_to_all | solution.py:88
  667.0 49.6 %all-to-all-done = f32[32,128,256]{2,0,1:T(8,128)} async-done(((f32[32,128,256]{2,0,1:T(8,128)}), f32[32,128,256]{2,0,1:T(8,128)}, u32[]{:S(2)}, u32[]{:S(2)}) %all-to-all-start) | async-done | bytes 4194336 | tf_op jit(solution)/shard_map/all_to_all | solution.py:88
  716.6 5.3 copy.37
  721.9 5.4 copy.38
  (317 shorter events, 256.4 us)
Async XLA Ops:
  7.2 468.9 %copy-start = (f32[65536]{0:T(1024)S(1)}, f32[65536]{0:T(1024)}, u32[]{:S(2)}) copy-start(f32[65536]{0:T(1024)} %param.12) | copy-start | bytes 786436
  7.2 559.4 %all-reduce.3.cloned.1.call-start = ((), (), s32[]{:S(2)}) async-start(), calls=%async_computation.1 | async-start | bytes 131072 | tf_op jit(solution)/shard_map/psum | solution.py:68
  385.6 5.3 copy-start.2
  385.6 5.4 copy-start.3
  655.1 61.5 %all-to-all-start = ((f32[32,128,256]{2,0,1:T(8,128)}), f32[32,128,256]{2,0,1:T(8,128)}, u32[]{:S(2)}, u32[]{:S(2)}) async-start(f32[32,128,256]{2,0,1:T(8,128)} %copy.36), calls=%async_computation | async-start | bytes 8388608 | tf_op jit(solution)/shard_map/all_to_all | solution.py:88
  721.9 5.4 copy-start.1
Sparse Core Ops, SparseCore 0:
  391.0 81.1 all-reduce.2
where the time goes:
time: 741 us; the launch traced here: 734 us
  local copies, waits for them, and re-layouts  368 us (50%)
  other arithmetic  197 us (27%)
  matrix products  92.8 us (13%)
  waiting for transfers between devices  49.6 us (7%)
  between operations  14.2 us (2%)
  starting transfers between devices  11.3 us (2%)
    scatter-add x1, other arithmetic, local(): jnp.zeros((width_slice, dirty_count), jnp.float32).at[:, slots[0]]  178 us
    gather x192, local copies, waits for them, and re-layouts  149 us
    gather x1, local copies, waits for them, and re-layouts, local(): accum_old = accum[dirty_local]  90.5 us
    gather x1, local copies, waits for them, and re-layouts, local(): old_rows = jnp.take(table, dirty_local, axis=1)  64.9 us
    dot_general x16, matrix products, place_columns(): jnp.dot(values, picker, precision=lax.Precision.HIGHEST, preferred_elemen...  61.4 us
    all_to_all x1, waiting for transfers between devices, local(): lax.all_to_all(buffer, ('row', 'col'), split_axis=1, concat_axis=0, tiled...  49.6 us
    unnamed x13, local copies, waits for them, and re-layouts  33.4 us
    dot_general x8, matrix products, one_block(): jnp.dot(piece, picker, precision=lax.Precision.HIGHEST, preferred_element...  30.7 us
  transfers between devices with their start and end apart: 2, of which 1 were waited for; matrix products, arithmetic and copies ran while one was open for 24% of the time, Pallas kernels for 0%

commit v1 on v0

v1 whole, which is shorter than its diff:
```python
import jax
import jax.numpy as jnp
from jax import lax
from jax.experimental import pallas as pl
from jax.experimental.pallas import tpu as pltpu
from jax.sharding import PartitionSpec as P

learn_rate = 0.3
epsilon = 1e-08

LANES = 128
CAP = 256
CHUNK = 512
BAGS = 64
LOW = 256
VMEM_LIMIT = 48 * 1024 * 1024

f32, bf16, i32 = jnp.float32, jnp.bfloat16, jnp.int32
NT = (((1,), (1,)), ((), ()))
NN = (((1,), (0,)), ((), ()))


def split(x):
    high = x.astype(bf16)
    return high, (x - high.astype(f32)).astype(bf16)


def params(limit=VMEM_LIMIT):
    return pltpu.CompilerParams(vmem_limit_bytes=limit)


def plan_body(row_ref, row_col_ref, own_ref, own_col_ref, accum_ref, srt_ref, tgt_ref, tgt_srt_ref, acc_ref):
    n = row_ref.shape[1]
    step = 256
    row, own = row_ref[...], own_ref[...]
    place = jnp.zeros((1, n), i32)
    srt = jnp.zeros((1, n), i32)
    tgt_srt = jnp.zeros((1, n), i32)
    lane = lax.broadcasted_iota(i32, (step, n), 1)
    for i in range(0, n, step):
        rows = row_col_ref[i : i + step, :]
        owns = own_col_ref[i : i + step, :]
        at = lax.broadcasted_iota(i32, (step, n), 0) + i
        rank = jnp.sum(jnp.where(row < rows, 1.0, 0.0), axis=1, keepdims=True).astype(i32)
        same = own == owns
        places = jnp.sum(
            jnp.where(same & (lane < at), 1.0, 0.0), axis=1, keepdims=True
        ).astype(i32)
        hit = rank == lane
        srt = srt + jnp.sum(jnp.where(hit, rows, 0), axis=0, keepdims=True)
        tgt_srt = tgt_srt + jnp.sum(
            jnp.where(hit, owns * CAP + places, 0), axis=0, keepdims=True
        )
        place = place + jnp.sum(jnp.where(same & (at < lane), 1, 0), axis=0, keepdims=True)
    srt_ref[...] = srt
    tgt_srt_ref[...] = tgt_srt
    tgt_ref[...] = own * CAP + place
    tall = accum_ref.shape[1]
    picker = jnp.where(
        lax.broadcasted_iota(i32, (tall, n), 0) == row // LANES, 1.0, 0.0
    )
    wide = lax.dot_general(
        accum_ref[...], picker, NN, precision=lax.Precision.HIGHEST, preferred_element_type=f32
    )
    keep = lax.broadcasted_iota(i32, (LANES, n), 0) == row % LANES
    acc_ref[...] = jnp.sum(jnp.where(keep, wide, 0.0), axis=0, keepdims=True)


def plan(rows, owners, accum):
    n = rows.shape[0]
    out = jax.ShapeDtypeStruct((1, n), i32)
    return pl.pallas_call(
        plan_body,
        out_shape=(out, out, out, jax.ShapeDtypeStruct((1, n), f32)),
        compiler_params=params(),
        name="plan",
    )(
        rows[None, :],
        rows[:, None],
        owners[None, :],
        owners[:, None],
        accum.reshape(-1, LANES).T,
    )


def counts_body(first_ref, last_ref, block_ref, bag_ref, slot_ref, out_ref):
    highs, bags, low = out_ref.shape
    span = highs * low
    rows = highs * BAGS
    chunks, chunk = bag_ref.shape

    def clear(i, carry):
        for h in range(highs):
            out_ref[h, pl.ds(pl.multiple_of(i * BAGS, BAGS), BAGS), :] = jnp.zeros(
                (BAGS, low), bf16
            )
        return carry

    lax.fori_loop(0, bags // BAGS, clear, 0)
    start = block_ref[0] * span
    left_iota = lax.broadcasted_iota(i32, (rows, chunk), 0)
    right_iota = lax.broadcasted_iota(i32, (low, chunk), 0)

    def one_chunk(i, carry):
        slot = slot_ref[pl.ds(i, 1), :] - start
        bag = bag_ref[pl.ds(i, 1), :]
        inside = (slot >= 0) & (slot < span)
        right = jnp.where(right_iota == (slot & (low - 1)), 1.0, 0.0).astype(bf16)
        base = jnp.where(inside, (slot // low) * BAGS, -(1 << 20))

        def one_window(w, carry):
            near = bag - w * BAGS
            left_id = jnp.where((near >= 0) & (near < BAGS), base + near, -1)
            left = jnp.where(left_iota == left_id, 1.0, 0.0).astype(bf16)
            both = lax.dot_general(left, right, NT, preferred_element_type=f32)
            at = pl.ds(pl.multiple_of(w * BAGS, BAGS), BAGS)
            for h in range(highs):
                piece = both[h * BAGS : (h + 1) * BAGS].astype(bf16)
                out_ref[h, at, :] = out_ref[h, at, :] + piece
            return carry

        return lax.fori_loop(first_ref[i], last_ref[i] + 1, one_window, carry)

    lax.fori_loop(0, chunks, one_chunk, 0)


def pair_counts(bag_of, slots, block, bags, span):
    chunks = bag_of.shape[0] // CHUNK
    bag = bag_of.reshape(chunks, CHUNK)
    smem = pl.BlockSpec(memory_space=pltpu.SMEM)
    vmem = pl.BlockSpec(memory_space=pltpu.VMEM)
    return pl.pallas_call(
        counts_body,
        out_shape=jax.ShapeDtypeStruct((span // LOW, bags, LOW), bf16),
        in_specs=[smem, smem, smem, vmem, vmem],
        out_specs=vmem,
        compiler_params=params(),
        cost_estimate=pl.CostEstimate(flops=int(8e9), bytes_accessed=5 << 20, transcendentals=0),
        name="pair_counts",
    )(
        bag[:, 0] // BAGS,
        bag[:, CHUNK - 1] // BAGS,
        block[None],
        bag,
        slots.reshape(chunks, CHUNK),
    )


UNROLL = 8


def gather_body(first_ref, last_ref, srt_ref, table_ref, out_ref):
    width, columns = table_ref.shape
    tiles = srt_ref.shape[1]
    groups = width // 8
    top = columns // LANES - 1
    block = pl.program_id(0)

    for t in range(tiles):
        row = srt_ref[0, t : t + 1, :]
        lane = jnp.broadcast_to(row % LANES, (8, LANES))
        tile = jnp.broadcast_to(row // LANES, (8, LANES))
        first = first_ref[block, t]
        steps = (last_ref[block, t] - first) // UNROLL + 1

        def step(i, accs):
            accs = list(accs)
            for u in range(UNROLL):
                v = jnp.minimum(first + i * UNROLL + u, top)
                at = pl.ds(pl.multiple_of(v * LANES, LANES), LANES)
                here = tile == v
                for g in range(groups):
                    part = table_ref[g * 8 : (g + 1) * 8, at]
                    picked = jnp.take_along_axis(part, lane, axis=1, mode="promise_in_bounds")
                    accs[g] = jnp.where(here, picked, accs[g])
            return tuple(accs)

        zero = jnp.zeros((8, LANES), f32)
        accs = lax.fori_loop(0, steps, step, (zero,) * groups)
        for g in range(groups):
            out_ref[0, g * 8 : (g + 1) * 8, t * LANES : (t + 1) * LANES] = accs[g]


def gather_rows(table, srt):
    width = table.shape[0]
    blocks, n = srt.shape
    tiles = n // LANES
    srt = srt.reshape(blocks, tiles, LANES)
    return pl.pallas_call(
        gather_body,
        grid_spec=pltpu.PrefetchScalarGridSpec(
            num_scalar_prefetch=2,
            grid=(blocks,),
            in_specs=[
                pl.BlockSpec((1, tiles, LANES), lambda b, *_: (b, 0, 0)),
                pl.BlockSpec(table.shape, lambda b, *_: (0, 0)),
            ],
            out_specs=pl.BlockSpec((1, width, n), lambda b, *_: (b, 0, 0)),
        ),
        out_shape=jax.ShapeDtypeStruct((blocks, width, n), f32),
        compiler_params=params(),
        cost_estimate=pl.CostEstimate(flops=int(1e9), bytes_accessed=10 << 20, transcendentals=0),
        name="gather_rows",
    )(srt[:, :, 0] // LANES, srt[:, :, LANES - 1] // LANES, srt, table)


def step_body(grad_ref, count_ref, old_ref, step_ref, new_ref, high_ref, low_ref):
    width = grad_ref.shape[0]
    tile = 128

    @pl.when(pl.program_id(0) == 0)
    def _():
        def cut(i, carry):
            at = pl.ds(pl.multiple_of(i * 32, 32), 32)
            high_ref[at, :], low_ref[at, :] = split(grad_ref[at, :])
            return carry

        lax.fori_loop(0, width // 32, cut, 0)

    count = count_ref[0]

    def one(i, total):
        at = pl.ds(pl.multiple_of(i * tile, tile), tile)
        grads = lax.dot_general(high_ref[at, :], count, NN, preferred_element_type=f32)
        grads = grads + lax.dot_general(low_ref[at, :], count, NN, preferred_element_type=f32)
        step_ref[at, :] = grads
        return total + jnp.sum(grads * grads, axis=0, keepdims=True)

    low = count.shape[1]
    total = lax.fori_loop(0, width // tile, one, jnp.zeros((1, low), f32))
    new = old_ref[...] + total / width
    new_ref[...] = new
    factor = learn_rate / (jnp.sqrt(new) + epsilon)
    step_ref[...] = step_ref[...] * factor


def steps_of(grad, count, old):
    width, bags = grad.shape
    highs, _, low = count.shape
    return pl.pallas_call(
        step_body,
        grid=(highs,),
        in_specs=[
            pl.BlockSpec((width, bags), lambda h: (0, 0)),
            pl.BlockSpec((1, bags, low), lambda h: (h, 0, 0)),
            pl.BlockSpec((1, low), lambda h: (0, h)),
        ],
        out_specs=[
            pl.BlockSpec((width, low), lambda h: (0, h)),
            pl.BlockSpec((1, low), lambda h: (0, h)),
        ],
        out_shape=(
            jax.ShapeDtypeStruct((width, highs * low), f32),
            jax.ShapeDtypeStruct((1, highs * low), f32),
        ),
        scratch_shapes=[pltpu.VMEM((width, bags), bf16), pltpu.VMEM((width, bags), bf16)],
        compiler_params=params(),
        cost_estimate=pl.CostEstimate(flops=int(8e9), bytes_accessed=10 << 20, transcendentals=0),
        name="steps_of",
    )(grad, count, old)


def place_body(old_ref, step_ref, tgt_srt_ref, tgt_ref, out_ref, oh_ref, ol_ref, sh_ref, sl_ref):
    width, n = old_ref.shape
    tile = 256

    @pl.when(pl.program_id(0) == 0)
    def _():
        def cut(i, carry):
            at = pl.ds(pl.multiple_of(i * 32, 32), 32)
            oh_ref[at, :], ol_ref[at, :] = split(old_ref[at, :])
            sh_ref[at, :], sl_ref[at, :] = split(-step_ref[at, :])
            return carry

        lax.fori_loop(0, width // 32, cut, 0)

    slot = lax.broadcasted_iota(i32, (CAP, n), 0) + pl.program_id(0) * CAP
    old_at = jnp.where(slot == tgt_srt_ref[...], 1.0, 0.0).astype(bf16)
    step_at = jnp.where(slot == tgt_ref[...], 1.0, 0.0).astype(bf16)

    def one(i, carry):
        at = pl.ds(pl.multiple_of(i * tile, tile), tile)
        total = lax.dot_general(oh_ref[at, :], old_at, NT, preferred_element_type=f32)
        total = total + lax.dot_general(ol_ref[at, :], old_at, NT, preferred_element_type=f32)
        total = total + lax.dot_general(sh_ref[at, :], step_at, NT, preferred_element_type=f32)
        total = total + lax.dot_general(sl_ref[at, :], step_at, NT, preferred_element_type=f32)
        out_ref[0, at, :] = total
        return carry

    lax.fori_loop(0, width // tile, one, 0)


def place(old, step, tgt_srt, tgt, owners):
    width, n = old.shape
    whole = lambda shape: pl.BlockSpec(shape, lambda o: (0, 0))
    return pl.pallas_call(
        place_body,
        grid=(owners,),
        in_specs=[whole((width, n)), whole((width, n)), whole((1, n)), whole((1, n))],
        out_specs=pl.BlockSpec((1, width, CAP), lambda o: (o, 0, 0)),
        out_shape=jax.ShapeDtypeStruct((owners, width, CAP), f32),
        scratch_shapes=[pltpu.VMEM((width, n), bf16)] * 4,
        compiler_params=params(),
        cost_estimate=pl.CostEstimate(flops=int(8e9), bytes_accessed=8 << 20, transcendentals=0),
        name="place",
    )(old, step, tgt_srt, tgt)


def local(table, accum, grad_pooled, bag_of, slots, dirty_rows, owner):
    width_slice, bags = grad_pooled.shape
    col_count = lax.axis_size("col")
    row_count = lax.axis_size("row")
    col = lax.axis_index("col")
    n = dirty_rows.shape[1] // col_count
    rows = lax.dynamic_slice_in_dim(dirty_rows[0], col * n, n)
    owners = lax.dynamic_slice_in_dim(owner[:, 0], col * n, n)
    grad = lax.all_gather(grad_pooled, "col", axis=0, tiled=True)
    srt, tgt, tgt_srt, accum_old = plan(rows, owners, accum)
    srt_all = lax.all_gather(srt[0], "col", axis=0)
    count = pair_counts(bag_of[0], slots[0], col, bags, n)
    picked = gather_rows(table, srt_all)
    old = lax.all_to_all(picked, "col", 0, 0, tiled=True)
    old = old.reshape(width_slice * col_count, n)
    step, accum_new = steps_of(grad, count, accum_old)
    placed = place(old, step, tgt_srt, tgt, row_count)
    received = lax.all_to_all(placed, "row", 0, 0, tiled=True)
    owned = jnp.transpose(received, (1, 0, 2)).reshape(width_slice * col_count, row_count * CAP)
    return owned, accum_new[0]


def solution(mesh):
    return jax.shard_map(
        local,
        mesh=mesh,
        in_specs=(
            P("col", "row"),
            P("row"),
            P("col", "row"),
            P("row", None),
            P("row", None),
            P("row", None),
            P("row", None),
        ),
        out_specs=(P(None, ("row", "col")), P(("row", "col"))),
        check_vma=False,
    )
```

time: 741 us -> 302 us (0.41)
  local copies, waits for them, and re-layouts: 368 us -> 19.7 us
  other arithmetic: 197 us -> 1.94 us
  Pallas kernels: 0 us -> 180 us
  matrix products: 92.8 us -> 0 us
  blocking collectives: 0 us -> 78.7 us
  waiting for transfers between devices: 49.6 us -> 0.69 us
    gather x194 -> x0, local copies, waits for them, and re-layouts: 304 us -> none
    pallas_call x0 -> x5, Pallas kernels: none -> 180 us  [the longest x1 120 us: gather_rows(): pl.pallas_call(gather_body, grid_spec=pltpu.PrefetchScalarGridSpec(num_sc...]
    scatter-add x1 -> x0, other arithmetic: 178 us -> none  [local(): jnp.zeros((width_slice, dirty_count), jnp.float32).at[:, slots[0]]]
    dot_general x25 -> x0, matrix products: 92.8 us -> none  [the longest x16 61.4 us: place_columns(): jnp.dot(values, picker, precision=lax.Precision.HIGHEST, preferred_elemen...]
    all_to_all x0 -> x1, blocking collectives: none -> 58.8 us  [local(): received = lax.all_to_all(placed, 'row', 0, 0, tiled=True)]
    all_to_all x1, waiting for transfers between devices: 49.6 us -> 0.01 us  [local(): old = lax.all_to_all(picked, 'col', 0, 0, tiled=True)]
    unnamed x13 -> x15, local copies, waits for them, and re-layouts: 33.4 us -> 11 us
    all_gather x0 -> x1, blocking collectives: none -> 19.9 us  [local(): srt_all = lax.all_gather(srt[0], 'col', axis=0)]
  transfers between devices with their start and end apart: 2 -> 2, of which waited for: 1 -> 0; matrix products, arithmetic and copies ran while one was open for 24% -> 2% of each run, Pallas kernels for 0% -> 55%
where the time goes in v1:
time: 302 us; the launch traced here: 301 us
  Pallas kernels  180 us (60%)
  blocking collectives  78.7 us (26%)
  local copies, waits for them, and re-layouts  19.7 us (7%)
  between operations  14.2 us (5%)
  starting transfers between devices  5.45 us (2%)
    pallas_call x1, Pallas kernels, gather_rows(): pl.pallas_call(gather_body, grid_spec=pltpu.PrefetchScalarGridSpec(num_sc...  120 us
    all_to_all x1, blocking collectives, local(): received = lax.all_to_all(placed, 'row', 0, 0, tiled=True)  58.8 us
    pallas_call x1, Pallas kernels, pair_counts(): pl.pallas_call(counts_body, out_shape=jax.ShapeDtypeStruct((span // LOW,...  30.8 us
    all_gather x1, blocking collectives, local(): srt_all = lax.all_gather(srt[0], 'col', axis=0)  19.9 us
    pallas_call x1, Pallas kernels, place(): pl.pallas_call(place_body, grid=(owners,), in_specs=[whole((width, n)), w...  13.8 us
    pallas_call x1, Pallas kernels, steps_of(): pl.pallas_call(step_body, grid=(highs,), in_specs=[pl.BlockSpec((width, b...  12 us
    unnamed x15, local copies, waits for them, and re-layouts  11 us
  transfers between devices with their start and end apart: 2, of which 0 were waited for; matrix products, arithmetic and copies ran while one was open for 2% of the time, Pallas kernels for 55%

profile of v1, /device:TPU:7, one launch (start us, length us, event | category | flops | bytes accessed | tf_op | source)
XLA Modules:
  0.0 301.0 jit_solution(717812691159515044)
XLA Ops:
  7.2 0.7 all-gather.3.cloned.1.call-update
  7.9 1.1 copy.36
  9.0 0.7 constant_dynamic-slice_fusion
  9.7 0.2 copy.52.own_col_ref
  10.0 0.2 copy.37.row_col_ref
  10.2 0.7 fusion.7.own_ref
  10.9 3.4 %plan.1 = (s32[1,1024]{1,0:T(1,128)S(1)}, s32[1,1024]{1,0:T(1,128)S(1)}, s32[1,1024]{1,0:T(1,128)S(1)}, f32[1,1024]{1,0:T(1,128)S(1)}) custom-call(s32[1,1024]{1,0:T(1,128)S(1)} %constant_dynamic-slice_fusion.1.row_ref, s32[1024,1]{1,0:T(8,128)S(1)} %copy.37.row_col_ref, s32[1,1024]{1,0:T(1,128)S(1)} %fusion.7.own_ref, s32[1024,1]{1,0:T(8,128)S(1)} %copy.52.own_col_ref, ...), custom_call_target="tpu_custom_call" | custom-call | tf_op jit(solution)/shard_map/plan/pallas_call | solution.py:72
  14.3 19.9 %all-gather = s32[16,1,1024]{2,1,0:T(1,128)S(1)} all-gather(s32[1,1,1024]{2,1,0:T(1,128)S(1)} %bitcast.52), channel_id=1, replica_groups=mesh['row'=8,'col'=16] {'col'}, dimensions={0}, use_global_device_ids=true | all-gather | bytes 69632 | tf_op jit(solution)/shard_map/all_gather | solution.py:319
  34.3 0.2 copy.51
  34.7 120.3 %gather_rows.1 = f32[16,32,1024]{2,1,0:T(8,128)} custom-call(s32[16,8]{1,0:T(8,128)S(1)} %get-tuple-element.25.first_ref, s32[16,8]{1,0:T(8,128)S(1)} %get-tuple-element.24.last_ref, s32[16,8,128]{2,1,0:T(8,128)S(1)} %bitcast.50, f32[32,65536]{1,0:T(8,128)} %table_ref.1), custom_call_target="tpu_custom_call" | custom-call | flops 1000000000 | bytes 10485760 | tf_op jit(solution)/shard_map/gather_rows/pallas_call | solution.py:189
  155.0 5.4 %all-to-all-start = ((f32[16,32,1024]{2,1,0:T(8,128)}), f32[16,32,1024]{2,1,0:T(8,128)S(1)}, u32[]{:S(2)}, u32[]{:S(2)}) async-start(f32[16,32,1024]{2,1,0:T(8,128)} %gather_rows.1), calls=%async_computation | async-start | bytes 4194304 | tf_op jit(solution)/shard_map/all_to_all | solution.py:322
  160.4 0.5 broadcast.39
  160.9 1.0 reduce.11
  161.9 1.0 reduce.12
  162.9 0.2 slice_reduce_fusion
  163.1 30.8 %pair_counts.1.count_ref = bf16[4,2048,256]{2,1,0:T(8,128)(2,1)S(1)} custom-call(s32[64]{0:T(128)S(1)} %get-tuple-element.23.first_ref, s32[64]{0:T(128)S(1)} %get-tuple-element.22.last_ref, s32[1]{0:T(128)} %bitcast.10.block_ref, s32[64,512]{1,0:T(8,128)S(1)} %reshape_squeeze.6.bag_ref, s32[64,512]{1,0:T(8,128)S(1)} %reshape_squeeze.7.slot_ref), custom_call_target="tpu_custom_call" | custom-call | flops 8000000000 | bytes 5242880 | tf_op jit(solution)/shard_map/pair_counts/pallas_call | solution.py:132
  193.9 2.0 copy-done.1
  195.9 12.0 %steps_of.1 = (f32[512,1024]{1,0:T(8,128)S(1)}, f32[1,1024]{1,0:T(1,128)}) custom-call(f32[512,2048]{1,0:T(8,128)} %all-gather.3.cloned.1.call-done.grad_ref, bf16[4,2048,256]{2,1,0:T(8,128)(2,1)} %copy-done.1, f32[1,1024]{1,0:T(1,128)S(1)} %get-tuple-element.9.old_ref), custom_call_target="tpu_custom_call" | custom-call | flops 8000000000 | bytes 10485760 | tf_op jit(solution)/shard_map/steps_of/pallas_call | solution.py:240
  207.9 1.3 copy-done.2
  209.2 1.6 copy-done.3
  210.8 13.8 %place.1 = f32[8,512,256]{2,1,0:T(8,128)} custom-call(f32[512,1024]{1,0:T(8,128)S(1)} %bitcast.48, f32[512,1024]{1,0:T(8,128)S(1)} %copy-done.3, s32[1,1024]{1,0:T(1,128)S(1)} %get-tuple-element.11.tgt_srt_ref, s32[1,1024]{1,0:T(1,128)S(1)} %get-tuple-element.12.tgt_ref), custom_call_target="tpu_custom_call" | custom-call | flops 8000000000 | bytes 8388608 | tf_op jit(solution)/shard_map/place/pallas_call | solution.py:296
  224.6 58.8 %all_to_all.10 = f32[8,512,256]{2,1,0:T(8,128)} all-to-all(f32[8,512,256]{2,1,0:T(8,128)} %place.1), channel_id=1, replica_groups=mesh['row'=8,'col'=16] {'row'}, dimensions={0} | all-to-all | bytes 8388608 | tf_op jit(solution)/shard_map/all_to_all | solution.py:326
  283.4 5.4 %copy.48 = f32[512,8,256]{0,2,1:T(8,128)} copy(f32[512,8,256]{2,0,1:T(8,128)} %bitcast.53) | data formatting | bytes 8388608 | tf_op jit(solution)/shard_map/transpose | solution.py:327
  288.8 5.3 %copy.49 = f32[512,2048]{1,0:T(8,128)} copy(f32[512,2048]{0,1:T(8,128)} %bitcast.54) | data formatting | bytes 8388608
  (20 shorter events, 0.4 us)
Async XLA Ops:
  7.2 2.8 copy-start
  7.2 188.7 %all-gather.3.cloned.1.call-start = ((), (), s32[]{:S(2)}) async-start(), calls=%async_computation.2 | async-start | bytes 4456448 | tf_op jit(solution)/shard_map/all_gather | solution.py:317
  155.0 5.9 %copy-start.4 = (s32[1,32768]{1,0:T(1,128)S(1)}, s32[1,32768]{1,0:T(1,128)}, u32[]{:S(2)}) copy-start(s32[1,32768]{1,0:T(1,128)} %param.10) | copy-start | bytes 393220
  155.0 6.9 %copy-start.5 = (s32[1,32768]{1,0:T(1,128)S(1)}, s32[1,32768]{1,0:T(1,128)}, u32[]{:S(2)}) copy-start(s32[1,32768]{1,0:T(1,128)} %param.11) | copy-start | bytes 393220
  155.0 54.2 %all-to-all-start = ((f32[16,32,1024]{2,1,0:T(8,128)}), f32[16,32,1024]{2,1,0:T(8,128)S(1)}, u32[]{:S(2)}, u32[]{:S(2)}) async-start(f32[16,32,1024]{2,1,0:T(8,128)} %gather_rows.1), calls=%async_computation | async-start | bytes 4194304 | tf_op jit(solution)/shard_map/all_to_all | solution.py:322
  193.9 2.0 copy-start.1
  207.9 1.3 copy-start.2
  209.2 1.6 copy-start.3
Sparse Core Ops, SparseCore 0:
  10.2 54.1 all-gather.2

commit v2 on v1

v2 whole, which is shorter than its diff:
```python
import jax
import jax.numpy as jnp
from jax import lax
from jax.experimental import pallas as pl
from jax.experimental.pallas import tpu as pltpu
from jax.sharding import PartitionSpec as P

learn_rate = 0.3
epsilon = 1e-08

LANES = 128
CAP = 256
CHUNK = 512
BAGS = 64
PAIRS = 5
LOW = 256
VMEM_LIMIT = 48 * 1024 * 1024

f32, bf16, i32 = jnp.float32, jnp.bfloat16, jnp.int32
NT = (((1,), (1,)), ((), ()))
NN = (((1,), (0,)), ((), ()))


def split(x):
    high = x.astype(bf16)
    return high, (x - high.astype(f32)).astype(bf16)


def params(limit=VMEM_LIMIT):
    return pltpu.CompilerParams(vmem_limit_bytes=limit)


def plan_body(row_ref, own_ref, own_col_ref, accum_ref, tgt_ref, acc_ref):
    n = row_ref.shape[1]
    step = 256
    row, own = row_ref[...], own_ref[...]
    place = jnp.zeros((1, n), i32)
    lane = lax.broadcasted_iota(i32, (step, n), 1)
    for i in range(0, n, step):
        at = lax.broadcasted_iota(i32, (step, n), 0) + i
        same = (own == own_col_ref[i : i + step, :]) & (at < lane)
        place = place + jnp.sum(jnp.where(same, 1, 0), axis=0, keepdims=True)
    tgt_ref[...] = own * CAP + place
    tall = accum_ref.shape[1]
    picker = jnp.where(
        lax.broadcasted_iota(i32, (tall, n), 0) == row // LANES, 1.0, 0.0
    )
    wide = lax.dot_general(
        accum_ref[...], picker, NN, precision=lax.Precision.HIGHEST, preferred_element_type=f32
    )
    keep = lax.broadcasted_iota(i32, (LANES, n), 0) == row % LANES
    acc_ref[...] = jnp.sum(jnp.where(keep, wide, 0.0), axis=0, keepdims=True)


def plan(rows, owners, accum):
    n = rows.shape[0]
    return pl.pallas_call(
        plan_body,
        out_shape=(jax.ShapeDtypeStruct((1, n), i32), jax.ShapeDtypeStruct((1, n), f32)),
        compiler_params=params(),
        name="plan",
    )(rows[None, :], owners[None, :], owners[:, None], accum.reshape(-1, LANES).T)


def counts_body(chunk_ref, window_ref, block_ref, bag_ref, slot_ref, out_ref):
    highs, bags, low = out_ref.shape
    span = highs * low
    rows = highs * BAGS
    pairs = chunk_ref.shape[0]
    chunk = bag_ref.shape[1]

    def clear(i, carry):
        for h in range(highs):
            out_ref[h, pl.ds(pl.multiple_of(i * BAGS, BAGS), BAGS), :] = jnp.zeros(
                (BAGS, low), bf16
            )
        return carry

    lax.fori_loop(0, bags // BAGS, clear, 0)
    start = block_ref[0] * span
    left_iota = lax.broadcasted_iota(i32, (rows, chunk), 0).astype(f32).astype(bf16)
    right_iota = lax.broadcasted_iota(i32, (low, chunk), 0).astype(f32).astype(bf16)
    one, zero = jnp.ones((), bf16), jnp.zeros((), bf16)

    def some(j, carry):
        done = []
        for u in range(PAIRS):
            i, w = chunk_ref[j * PAIRS + u], window_ref[j * PAIRS + u]
            slot = slot_ref[pl.ds(i, 1), :] - start
            near = bag_ref[pl.ds(i, 1), :] - w * BAGS
            inside = (slot >= 0) & (slot < span) & (near >= 0) & (near < BAGS)
            left_id = jnp.where(inside, (slot // low) * BAGS + near, -1)
            left_id = left_id.astype(f32).astype(bf16)
            right_id = (slot & (low - 1)).astype(f32).astype(bf16)
            left = jnp.where(left_iota == left_id, one, zero)
            right = jnp.where(right_iota == right_id, one, zero)
            done.append((w, lax.dot_general(left, right, NT, preferred_element_type=f32)))
        for w, both in done:
            at = pl.ds(pl.multiple_of(w * BAGS, BAGS), BAGS)
            for h in range(highs):
                piece = both[h * BAGS : (h + 1) * BAGS].astype(bf16)
                out_ref[h, at, :] = out_ref[h, at, :] + piece
        return carry

    lax.fori_loop(0, pairs // PAIRS, some, 0)


def pair_counts(bag_of, slots, block, bags, span):
    chunks = bag_of.shape[0] // CHUNK
    bag = bag_of.reshape(chunks, CHUNK)
    total = chunks + bags // BAGS - 1
    assert total % PAIRS == 0
    ends = jnp.arange(chunks, dtype=i32) + bag[:, CHUNK - 1] // BAGS
    order = jnp.arange(total, dtype=i32)
    at_chunk = jnp.sum((ends[None, :] < order[:, None]).astype(i32), axis=1)
    at_window = order - at_chunk
    smem = pl.BlockSpec(memory_space=pltpu.SMEM)
    vmem = pl.BlockSpec(memory_space=pltpu.VMEM)
    return pl.pallas_call(
        counts_body,
        out_shape=jax.ShapeDtypeStruct((span // LOW, bags, LOW), bf16),
        in_specs=[smem, smem, smem, vmem, vmem],
        out_specs=vmem,
        compiler_params=params(),
        cost_estimate=pl.CostEstimate(flops=int(8e9), bytes_accessed=5 << 20, transcendentals=0),
        name="pair_counts",
    )(at_chunk, at_window, block[None], bag, slots.reshape(chunks, CHUNK))


def gather_body(row_ref, part_ref, table_ref, out_ref, tall_ref, stage_ref):
    width, columns = table_ref.shape
    parts = LANES // width
    height = columns // parts
    blocks, _, n = out_ref.shape
    per = n // LANES
    tiles = blocks * per

    def turn(i, carry):
        at = pl.multiple_of(i * LANES, LANES)
        wide = [table_ref[:, pl.ds(pl.multiple_of(q * height + at, LANES), LANES)] for q in range(parts)]
        tall_ref[pl.ds(at, LANES), :] = jnp.concatenate(wide, axis=0).T
        return carry

    lax.fori_loop(0, height // LANES, turn, 0, unroll=2)

    def fetch(t, slot):
        for u in range(LANES):
            row = row_ref[t * LANES + u] & (height - 1)
            stage_ref[slot, u : u + 1, :] = tall_ref[pl.ds(row, 1), :]

    def emit(t, slot):
        flat = stage_ref[slot].T
        part = part_ref[pl.ds(t, 1), :] // height
        picked = flat[:width]
        for q in range(1, parts):
            picked = jnp.where(part == q, flat[q * width : (q + 1) * width], picked)
        at = pl.ds(pl.multiple_of((t % per) * LANES, LANES), LANES)
        out_ref[t // per, :, at] = picked

    fetch(0, 0)

    def two(i, carry):
        fetch(2 * i + 1, 1)
        emit(2 * i, 0)
        fetch(jnp.minimum(2 * i + 2, tiles - 1), 0)
        emit(2 * i + 1, 1)
        return carry

    lax.fori_loop(0, tiles // 2, two, 0)


def gather_rows(table, rows, blocks):
    width, columns = table.shape
    n = rows.shape[0] // blocks
    vmem = pl.BlockSpec(memory_space=pltpu.VMEM)
    return pl.pallas_call(
        gather_body,
        in_specs=[pl.BlockSpec(memory_space=pltpu.SMEM), vmem, vmem],
        out_specs=vmem,
        out_shape=jax.ShapeDtypeStruct((blocks, width, n), f32),
        scratch_shapes=[
            pltpu.VMEM((columns * width // LANES, LANES), f32),
            pltpu.VMEM((2, LANES, LANES), f32),
        ],
        compiler_params=params(),
        cost_estimate=pl.CostEstimate(flops=int(1e9), bytes_accessed=10 << 20, transcendentals=0),
        name="gather_rows",
    )(rows, rows.reshape(-1, LANES), table)


def step_body(grad_ref, count_ref, old_ref, step_ref, new_ref, high_ref, low_ref):
    width = grad_ref.shape[0]
    tile = 256

    @pl.when(pl.program_id(0) == 0)
    def _():
        def cut(i, carry):
            at = pl.ds(pl.multiple_of(i * 32, 32), 32)
            high_ref[at, :], low_ref[at, :] = split(grad_ref[at, :])
            return carry

        lax.fori_loop(0, width // 32, cut, 0)

    count = count_ref[0]

    def one(i, total):
        at = pl.ds(pl.multiple_of(i * tile, tile), tile)
        grads = lax.dot_general(high_ref[at, :], count, NN, preferred_element_type=f32)
        grads = grads + lax.dot_general(low_ref[at, :], count, NN, preferred_element_type=f32)
        step_ref[at, :] = grads
        return total + jnp.sum(grads * grads, axis=0, keepdims=True)

    low = count.shape[1]
    total = lax.fori_loop(0, width // tile, one, jnp.zeros((1, low), f32))
    new = old_ref[...] + total / width
    new_ref[...] = new
    factor = learn_rate / (jnp.sqrt(new) + epsilon)
    step_ref[...] = step_ref[...] * factor


def steps_of(grad, count, old):
    width, bags = grad.shape
    highs, _, low = count.shape
    return pl.pallas_call(
        step_body,
        grid=(highs,),
        in_specs=[
            pl.BlockSpec((width, bags), lambda h: (0, 0)),
            pl.BlockSpec((1, bags, low), lambda h: (h, 0, 0)),
            pl.BlockSpec((1, low), lambda h: (0, h)),
        ],
        out_specs=[
            pl.BlockSpec((width, low), lambda h: (0, h)),
            pl.BlockSpec((1, low), lambda h: (0, h)),
        ],
        out_shape=(
            jax.ShapeDtypeStruct((width, highs * low), f32),
            jax.ShapeDtypeStruct((1, highs * low), f32),
        ),
        scratch_shapes=[pltpu.VMEM((width, bags), bf16), pltpu.VMEM((width, bags), bf16)],
        compiler_params=params(),
        cost_estimate=pl.CostEstimate(flops=int(8e9), bytes_accessed=10 << 20, transcendentals=0),
        name="steps_of",
    )(grad, count, old)


def place_body(old_ref, step_ref, tgt_ref, out_ref, high_ref, low_ref):
    width, n = old_ref.shape
    tile = 256

    @pl.when(pl.program_id(0) == 0)
    def _():
        def cut(i, carry):
            at = pl.ds(pl.multiple_of(i * 32, 32), 32)
            high_ref[at, :], low_ref[at, :] = split(old_ref[at, :] - step_ref[at, :])
            return carry

        lax.fori_loop(0, width // 32, cut, 0)

    slot = lax.broadcasted_iota(i32, (CAP, n), 0) + pl.program_id(0) * CAP
    here = jnp.where(slot == tgt_ref[...], 1.0, 0.0).astype(bf16)

    def one(i, carry):
        at = pl.ds(pl.multiple_of(i * tile, tile), tile)
        total = lax.dot_general(high_ref[at, :], here, NT, preferred_element_type=f32)
        total = total + lax.dot_general(low_ref[at, :], here, NT, preferred_element_type=f32)
        out_ref[0, at, :] = total
        return carry

    lax.fori_loop(0, width // tile, one, 0)


def place(old, step, tgt, owners):
    width, n = old.shape
    whole = lambda shape: pl.BlockSpec(shape, lambda o: (0, 0))
    return pl.pallas_call(
        place_body,
        grid=(owners,),
        in_specs=[whole((width, n)), whole((width, n)), whole((1, n))],
        out_specs=pl.BlockSpec((1, width, CAP), lambda o: (o, 0, 0)),
        out_shape=jax.ShapeDtypeStruct((owners, width, CAP), f32),
        scratch_shapes=[pltpu.VMEM((width, n), bf16)] * 2,
        compiler_params=params(),
        cost_estimate=pl.CostEstimate(flops=int(4e9), bytes_accessed=8 << 20, transcendentals=0),
        name="place",
    )(old, step, tgt)


def join_body(part_ref, out_ref):
    out_ref[...] = part_ref[0]


def join(parts):
    count, width, cap = parts.shape
    return pl.pallas_call(
        join_body,
        grid=(count,),
        in_specs=[pl.BlockSpec((1, width, cap), lambda s: (s, 0, 0))],
        out_specs=pl.BlockSpec((width, cap), lambda s: (0, s)),
        out_shape=jax.ShapeDtypeStruct((width, count * cap), f32),
        name="join",
    )(parts)


def local(table, accum, grad_pooled, bag_of, slots, dirty_rows, owner):
    width_slice, bags = grad_pooled.shape
    col_count = lax.axis_size("col")
    row_count = lax.axis_size("row")
    col = lax.axis_index("col")
    n = dirty_rows.shape[1] // col_count
    rows = lax.dynamic_slice_in_dim(dirty_rows[0], col * n, n)
    owners = lax.dynamic_slice_in_dim(owner[:, 0], col * n, n)
    grad = lax.all_gather(grad_pooled, "col", axis=0, tiled=True)
    tgt, accum_old = plan(rows, owners, accum)
    picked = gather_rows(table, dirty_rows[0], col_count)
    old = lax.all_to_all(picked, "col", 0, 0, tiled=True)
    old = old.reshape(width_slice * col_count, n)
    count = pair_counts(bag_of[0], slots[0], col, bags, n)
    step, accum_new = steps_of(grad, count, accum_old)
    placed = place(old, step, tgt, row_count)
    owned = join(lax.all_to_all(placed, "row", 0, 0, tiled=True))
    return owned, accum_new[0]


def solution(mesh):
    return jax.shard_map(
        local,
        mesh=mesh,
        in_specs=(
            P("col", "row"),
            P("row"),
            P("col", "row"),
            P("row", None),
            P("row", None),
            P("row", None),
            P("row", None),
        ),
        out_specs=(P(None, ("row", "col")), P(("row", "col"))),
        check_vma=False,
    )
```

time: 302 us -> 176 us (0.58)
  Pallas kernels: 180 us -> 72.9 us
  blocking collectives: 78.7 us -> 54.4 us
  waiting for transfers between devices: 0.69 us -> 15.5 us
  local copies, waits for them, and re-layouts: 19.7 us -> 7.55 us
    pallas_call x2 -> x3, Pallas kernels: 124 us -> 41.8 us  [the longest x1 33.5 us: gather_rows(): pl.pallas_call(gather_body, in_specs=[pl.BlockSpec(memory_space=pltpu.SME...]
    all_gather x1 -> x0, blocking collectives: 19.9 us -> none  [local(): srt_all = lax.all_gather(srt[0], 'col', axis=0)]
    pallas_call x1, Pallas kernels: 30.8 us -> 11.9 us  [pair_counts(): pl.pallas_call(counts_body, out_shape=jax.ShapeDtypeStruct((span // LOW,...]
    all_gather x1, waiting for transfers between devices: 0.01 us -> 14.8 us  [local(): grad = lax.all_gather(grad_pooled, 'col', axis=0, tiled=True)]
    transpose x1 -> x0, local copies, waits for them, and re-layouts: 5.38 us -> none  [local(): jnp.transpose(received, (1, 0, 2))]
    pallas_call x1, Pallas kernels: 13.8 us -> 8.94 us  [place(): pl.pallas_call(place_body, grid=(owners,), in_specs=[whole((width, n)), w...]
    unnamed x15 -> x16, local copies, waits for them, and re-layouts: 11 us -> 6.5 us
    all_to_all x1, blocking collectives: 58.8 us -> 54.4 us  [local(): owned = join(lax.all_to_all(placed, 'row', 0, 0, tiled=True))]
  transfers between devices with their start and end apart: 2 -> 2, of which waited for: 0 -> 1; matrix products, arithmetic and copies ran while one was open for 2% -> 3% of each run, Pallas kernels for 55% -> 33%
where the time goes in v2:
time: 176 us; the launch traced here: 175 us
  Pallas kernels  72.9 us (41%)
  blocking collectives  54.4 us (31%)
  waiting for transfers between devices  15.5 us (9%)
  between operations  14.1 us (8%)
  starting transfers between devices  7.88 us (4%)
  local copies, waits for them, and re-layouts  7.55 us (4%)
  other arithmetic  2.93 us (2%)
    all_to_all x1, blocking collectives, local(): owned = join(lax.all_to_all(placed, 'row', 0, 0, tiled=True))  54.4 us
    pallas_call x1, Pallas kernels, gather_rows(): pl.pallas_call(gather_body, in_specs=[pl.BlockSpec(memory_space=pltpu.SME...  33.5 us
    all_gather x1, waiting for transfers between devices, local(): grad = lax.all_gather(grad_pooled, 'col', axis=0, tiled=True)  14.8 us
    pallas_call x1, Pallas kernels, pair_counts(): pl.pallas_call(counts_body, out_shape=jax.ShapeDtypeStruct((span // LOW,...  11.9 us
    pallas_call x1, Pallas kernels, steps_of(): pl.pallas_call(step_body, grid=(highs,), in_specs=[pl.BlockSpec((width, b...  10.3 us
    pallas_call x1, Pallas kernels, place(): pl.pallas_call(place_body, grid=(owners,), in_specs=[whole((width, n)), w...  8.94 us
    all_to_all x1, starting transfers between devices, local(): old = lax.all_to_all(picked, 'col', 0, 0, tiled=True)  7.84 us
    pallas_call x1, Pallas kernels, join(): pl.pallas_call(join_body, grid=(count,), in_specs=[pl.BlockSpec((1, width...  6.58 us
  transfers between devices with their start and end apart: 2, of which 1 were waited for; matrix products, arithmetic and copies ran while one was open for 3% of the time, Pallas kernels for 33%

profile of v2, /device:TPU:7, one launch (start us, length us, event | category | flops | bytes accessed | tf_op | source)
XLA Modules:
  0.0 175.3 jit_solution(8544608271721552910)
XLA Ops:
  7.2 0.0 copy-start
  7.2 0.0 all-gather.2.cloned.1.call-start
  7.2 0.7 all-gather.2.cloned.1.call-update
  7.9 0.8 copy-done.1
  8.8 33.5 %gather_rows.1 = f32[16,32,1024]{2,1,0:T(8,128)} custom-call(s32[16384]{0:T(1024)S(1)} %bitcast.12, s32[128,128]{1,0:T(8,128)S(1)} %bitcast.13, f32[32,65536]{1,0:T(8,128)} %table_ref.1), custom_call_target="tpu_custom_call" | custom-call | flops 1000000000 | bytes 10485760 | tf_op jit(solution)/shard_map/gather_rows/pallas_call | solution.py:176
  42.3 7.8 %all-to-all-start = ((f32[16,32,1024]{2,1,0:T(8,128)}), f32[16,32,1024]{2,1,0:T(8,128)S(1)}, u32[]{:S(2)}, u32[]{:S(2)}) async-start(f32[16,32,1024]{2,1,0:T(8,128)} %gather_rows.1), calls=%async_computation | async-start | bytes 4194304 | tf_op jit(solution)/shard_map/all_to_all | solution.py:316
  50.2 0.2 copy.14.own_col_ref
  50.4 0.1 copy.13
  50.5 0.5 broadcast.42
  51.1 1.0 reduce.9
  52.0 1.9 %reduce.10 = s32[32768]{0:T(1024)S(1)} reduce(s32[1,32768]{1,0:T(1,128)} %param.11, s32[]{:T(128)} %broadcast.42), dimensions={0}, to_apply=%param.11.reduce_sub_computation.3 | reduce | bytes 262148 | tf_op args[4]
  53.9 0.7 constant_dynamic-slice_fusion.1.row_ref
  54.6 1.6 plan.1
  56.3 0.2 slice_reduce_fusion
  56.5 0.1 convert_reduce_fusion.chunk_ref
  56.6 11.9 %pair_counts.1.count_ref = bf16[4,2048,256]{2,1,0:T(8,128)(2,1)S(1)} custom-call(s32[95]{0:T(128)S(1)} %convert_reduce_fusion.chunk_ref, s32[95]{0:T(128)S(1)} %iota_subtract_fusion.window_ref, s32[1]{0:T(128)} %bitcast.3.block_ref, s32[64,512]{1,0:T(8,128)S(1)} %reshape_squeeze.10.bag_ref, s32[64,512]{1,0:T(8,128)S(1)} %reshape_squeeze.11.slot_ref), custom_call_target="tpu_custom_call" | custom-call | flops 8000000000 | bytes 5242880 | tf_op jit(solution)/shard_map/pair_counts/pallas_call | solution.py:119
  68.5 2.0 %copy-done.4 = bf16[4,2048,256]{2,1,0:T(8,128)(2,1)} copy-done((bf16[4,2048,256]{2,1,0:T(8,128)(2,1)}, bf16[4,2048,256]{2,1,0:T(8,128)(2,1)S(1)}, u32[]{:S(2)}) %copy-start.4) | copy-done | bytes 4194328
  70.5 14.8 %all-gather.2.cloned.1.call-done.grad_ref = f32[512,2048]{1,0:T(8,128)} async-done(((f32[32,2048]{1,0:T(8,128)}), f32[512,2048]{1,0:T(8,128)}) %all-gather.2.cloned.1.call-update) | async-done | bytes 4194320 | tf_op jit(solution)/shard_map/all_gather | solution.py:313
  85.3 10.3 %steps_of.1 = (f32[512,1024]{1,0:T(8,128)S(1)}, f32[1,1024]{1,0:T(1,128)}) custom-call(f32[512,2048]{1,0:T(8,128)} %all-gather.2.cloned.1.call-done.grad_ref, bf16[4,2048,256]{2,1,0:T(8,128)(2,1)} %copy-done.4, f32[1,1024]{1,0:T(1,128)S(1)} %get-tuple-element.6.old_ref), custom_call_target="tpu_custom_call" | custom-call | flops 8000000000 | bytes 10485760 | tf_op jit(solution)/shard_map/steps_of/pallas_call | solution.py:224
  95.6 1.3 copy-done.2
  96.9 1.6 copy-done.3
  98.5 8.9 %place.1 = f32[8,512,256]{2,1,0:T(8,128)} custom-call(f32[512,1024]{1,0:T(8,128)S(1)} %bitcast.10, f32[512,1024]{1,0:T(8,128)S(1)} %copy-done.3, s32[1,1024]{1,0:T(1,128)S(1)} %get-tuple-element.8.tgt_ref), custom_call_target="tpu_custom_call" | custom-call | flops 4000000000 | bytes 8388608 | tf_op jit(solution)/shard_map/place/pallas_call | solution.py:276
  107.4 54.4 %all_to_all.10.part_ref = f32[8,512,256]{2,1,0:T(8,128)} all-to-all(f32[8,512,256]{2,1,0:T(8,128)} %place.1), channel_id=1, replica_groups=mesh['row'=8,'col'=16] {'row'}, dimensions={0} | all-to-all | bytes 8388608 | tf_op jit(solution)/shard_map/all_to_all | solution.py:321
  161.9 6.6 %join.1 = f32[512,2048]{1,0:T(8,128)} custom-call(f32[8,512,256]{2,1,0:T(8,128)} %all_to_all.10.part_ref), custom_call_target="tpu_custom_call" | custom-call | tf_op jit(solution)/shard_map/join/pallas_call | solution.py:295
  (16 shorter events, 0.1 us)
Async XLA Ops:
  7.2 43.0 %copy-start = (s32[16384,1]{0,1:T(1,128)S(1)}, s32[16384,1]{0,1:T(1,128)}, u32[]{:S(2)}) copy-start(s32[16384,1]{0,1:T(1,128)} %param.13) | copy-start | bytes 196612
  7.2 78.1 %all-gather.2.cloned.1.call-start = ((), (), s32[]{:S(2)}) async-start(), calls=%async_computation.2 | async-start | bytes 4456448 | tf_op jit(solution)/shard_map/all_gather | solution.py:313
  7.9 0.8 copy-start.1
  42.3 8.1 %copy-start.5 = (f32[65536]{0:T(1024)S(1)}, f32[65536]{0:T(1024)}, u32[]{:S(2)}) copy-start(f32[65536]{0:T(1024)} %param.8) | copy-start | bytes 786436
  42.3 8.8 %copy-start.6 = (s32[1,32768]{1,0:T(1,128)S(1)}, s32[1,32768]{1,0:T(1,128)}, u32[]{:S(2)}) copy-start(s32[1,32768]{1,0:T(1,128)} %param.10) | copy-start | bytes 393220
  42.3 54.6 %all-to-all-start = ((f32[16,32,1024]{2,1,0:T(8,128)}), f32[16,32,1024]{2,1,0:T(8,128)S(1)}, u32[]{:S(2)}, u32[]{:S(2)}) async-start(f32[16,32,1024]{2,1,0:T(8,128)} %gather_rows.1), calls=%async_computation | async-start | bytes 4194304 | tf_op jit(solution)/shard_map/all_to_all | solution.py:316
  68.5 2.0 %copy-start.4 = (bf16[4,2048,256]{2,1,0:T(8,128)(2,1)}, bf16[4,2048,256]{2,1,0:T(8,128)(2,1)S(1)}, u32[]{:S(2)}) copy-start(bf16[4,2048,256]{2,1,0:T(8,128)(2,1)S(1)} %pair_counts.1.count_ref) | copy-start | bytes 12582916
  95.6 1.3 copy-start.2
  96.9 1.6 copy-start.3
Sparse Core Ops, SparseCore 0:
  10.2 75.0 all-gather.1

commit v3 on v2

v3 whole, which is shorter than its diff:
```python
import functools

import jax
import jax.numpy as jnp
from jax import lax
from jax.experimental import pallas as pl
from jax.experimental.pallas import tpu as pltpu
from jax.sharding import PartitionSpec as P

learn_rate = 0.3
epsilon = 1e-08

LANES = 128
CAP = 256
CHUNK = 512
BAGS = 64
PAIRS = 5
LOW = 256
SHARES = 2

f32, bf16, i32 = jnp.float32, jnp.bfloat16, jnp.int32
NT = (((1,), (1,)), ((), ()))
NN = (((1,), (0,)), ((), ()))


def split(x):
    high = x.astype(bf16)
    return high, (x - high.astype(f32)).astype(bf16)


def params(mib):
    return pltpu.CompilerParams(vmem_limit_bytes=mib * 1024 * 1024)


SMEM = pl.BlockSpec(memory_space=pltpu.SMEM)
VMEM = pl.BlockSpec(memory_space=pltpu.VMEM)
ANY = pl.BlockSpec(memory_space=pl.ANY)
HBM = pl.BlockSpec(memory_space=pltpu.HBM)


def plan_body(col_ref, row_ref, own_ref, accum_ref, tgt_ref, acc_ref):
    n = row_ref.shape[1]
    row, own = row_ref[...], own_ref[...]
    named = jnp.where(lax.broadcasted_iota(i32, (8, n), 0) == own, 1.0, 0.0)
    earlier = lax.broadcasted_iota(i32, (n, n), 0) < lax.broadcasted_iota(i32, (n, n), 1)
    earlier = jnp.where(earlier, 1.0, 0.0).astype(bf16)
    before = lax.dot_general(named.astype(bf16), earlier, NN, preferred_element_type=f32)
    place = jnp.sum(named * before, axis=0, keepdims=True).astype(i32)
    tgt_ref[...] = own * CAP + place
    tall = accum_ref.shape[0]
    picker = jnp.where(
        lax.broadcasted_iota(i32, (tall, n), 0) == row // LANES, 1.0, 0.0
    )
    wide = lax.dot_general(
        accum_ref[...].T, picker, NN, precision=lax.Precision.HIGHEST, preferred_element_type=f32
    )
    keep = lax.broadcasted_iota(i32, (LANES, n), 0) == row % LANES
    acc_ref[...] = jnp.sum(jnp.where(keep, wide, 0.0), axis=0, keepdims=True)


def plan(col, rows, owners, accum, blocks):
    assert blocks % 8 == 0
    n = rows.shape[1] // blocks
    accum = accum.reshape(-1, LANES)
    own = lambda i, c: (0, c[0])
    return pl.pallas_call(
        plan_body,
        grid_spec=pltpu.PrefetchScalarGridSpec(
            num_scalar_prefetch=1,
            grid=(1,),
            in_specs=[
                pl.BlockSpec((1, n), own),
                pl.BlockSpec((1, n), own),
                pl.BlockSpec(accum.shape, lambda i, c: (0, 0)),
            ],
            out_specs=[pl.BlockSpec((1, n), lambda i, c: (0, 0))] * 2,
        ),
        out_shape=(jax.ShapeDtypeStruct((1, n), i32), jax.ShapeDtypeStruct((1, n), f32)),
        compiler_params=params(16),
        name="plan",
    )(col[None], rows, owners, accum)


def counts_body(block_ref, end_ref, bag_ref, slot_ref, out_ref):
    highs, bags, low = out_ref.shape
    span = highs * low
    rows = highs * BAGS
    chunks = bag_ref.shape[1] // CHUNK
    pairs = chunks + bags // BAGS - 1
    assert pairs % PAIRS == 0

    def clear(i, carry):
        for h in range(highs):
            out_ref[h, pl.ds(pl.multiple_of(i * BAGS, BAGS), BAGS), :] = jnp.zeros(
                (BAGS, low), bf16
            )
        return carry

    lax.fori_loop(0, bags // BAGS, clear, 0)
    start = block_ref[0] * span
    left_iota = lax.broadcasted_iota(i32, (rows, CHUNK), 0).astype(f32).astype(bf16)
    right_iota = lax.broadcasted_iota(i32, (low, CHUNK), 0).astype(f32).astype(bf16)
    one, zero = jnp.ones((), bf16), jnp.zeros((), bf16)

    def some(j, carry):
        i, w = carry
        done = []
        for u in range(PAIRS):
            at = pl.ds(pl.multiple_of(i * CHUNK, CHUNK), CHUNK)
            slot = slot_ref[:, at] - start
            near = bag_ref[:, at] - w * BAGS
            inside = (slot >= 0) & (slot < span) & (near >= 0) & (near < BAGS)
            left_id = jnp.where(inside, (slot // low) * BAGS + near, -1)
            left_id = left_id.astype(f32).astype(bf16)
            right_id = (slot & (low - 1)).astype(f32).astype(bf16)
            left = jnp.where(left_iota == left_id, one, zero)
            right = jnp.where(right_iota == right_id, one, zero)
            done.append((w, lax.dot_general(left, right, NT, preferred_element_type=f32)))
            more = w < end_ref[0, i * CHUNK + CHUNK - 1] // BAGS
            i, w = (
                jnp.where(more, i, jnp.minimum(i + 1, chunks - 1)),
                jnp.where(more, w + 1, w),
            )
        for v, both in done:
            at = pl.ds(pl.multiple_of(v * BAGS, BAGS), BAGS)
            for h in range(highs):
                piece = both[h * BAGS : (h + 1) * BAGS].astype(bf16)
                out_ref[h, at, :] = out_ref[h, at, :] + piece
        return i, w

    lax.fori_loop(0, pairs // PAIRS, some, (0, 0))


def pair_counts(bag_of, slots, block, bags, span):
    smem = pl.BlockSpec(memory_space=pltpu.SMEM)
    vmem = pl.BlockSpec(memory_space=pltpu.VMEM)
    return pl.pallas_call(
        counts_body,
        out_shape=jax.ShapeDtypeStruct((span // LOW, bags, LOW), bf16),
        in_specs=[smem, smem, vmem, vmem],
        out_specs=vmem,
        compiler_params=params(12),
        cost_estimate=pl.CostEstimate(flops=int(8e9), bytes_accessed=5 << 20, transcendentals=0),
        name="pair_counts",
    )(block[None], bag_of, bag_of, slots)


def gather_body(row_ref, part_ref, table_ref, after_ref, *refs):
    out_refs, (tall_ref, stage_ref) = refs[:SHARES], refs[SHARES:]
    width, columns = table_ref.shape
    parts = LANES // width
    height = columns // parts
    blocks, narrow, n = out_refs[0].shape
    per = n // LANES
    tiles = blocks * per

    def turn(i, carry):
        at = pl.multiple_of(i * LANES, LANES)
        wide = [table_ref[:, pl.ds(pl.multiple_of(q * height + at, LANES), LANES)] for q in range(parts)]
        tall_ref[pl.ds(at, LANES), :] = jnp.concatenate(wide, axis=0).T
        return carry

    lax.fori_loop(0, height // LANES, turn, 0, unroll=2)

    def fetch(t, slot):
        for u in range(LANES):
            row = row_ref[0, t * LANES + u] & (height - 1)
            stage_ref[slot, u : u + 1, :] = tall_ref[pl.ds(row, 1), :]

    def emit(t, slot):
        flat = stage_ref[slot].T
        part = part_ref[:, pl.ds(pl.multiple_of(t * LANES, LANES), LANES)] // height
        picked = flat[:width]
        for q in range(1, parts):
            picked = jnp.where(part == q, flat[q * width : (q + 1) * width], picked)
        at = pl.ds(pl.multiple_of((t % per) * LANES, LANES), LANES)
        for h, out_ref in enumerate(out_refs):
            out_ref[t // per, :, at] = picked[h * narrow : (h + 1) * narrow]

    fetch(0, 0)

    def two(i, carry):
        fetch(2 * i + 1, 1)
        emit(2 * i, 0)
        fetch(jnp.minimum(2 * i + 2, tiles - 1), 0)
        emit(2 * i + 1, 1)
        return carry

    lax.fori_loop(0, tiles // 2, two, 0)


def gather_rows(table, rows, blocks, after):
    width, columns = table.shape
    n = rows.shape[1] // blocks
    return pl.pallas_call(
        gather_body,
        in_specs=[SMEM, VMEM, VMEM, ANY],
        out_specs=[VMEM] * SHARES,
        out_shape=(jax.ShapeDtypeStruct((blocks, width // SHARES, n), f32),) * SHARES,
        scratch_shapes=[
            pltpu.VMEM((columns * width // LANES, LANES), f32),
            pltpu.VMEM((2, LANES, LANES), f32),
        ],
        compiler_params=params(24),
        cost_estimate=pl.CostEstimate(flops=int(1e9), bytes_accessed=10 << 20, transcendentals=0),
        name="gather_rows",
    )(rows, rows, table, after)


def step_body(grad_ref, count_ref, old_ref, step_ref, new_ref, high_ref, low_ref):
    width = grad_ref.shape[0]
    tile = 256

    @pl.when(pl.program_id(0) == 0)
    def _():
        def cut(i, carry):
            at = pl.ds(pl.multiple_of(i * 32, 32), 32)
            high_ref[at, :], low_ref[at, :] = split(grad_ref[at, :])
            return carry

        lax.fori_loop(0, width // 32, cut, 0)

    count = count_ref[0]

    def one(i, total):
        at = pl.ds(pl.multiple_of(i * tile, tile), tile)
        grads = lax.dot_general(high_ref[at, :], count, NN, preferred_element_type=f32)
        grads = grads + lax.dot_general(low_ref[at, :], count, NN, preferred_element_type=f32)
        step_ref[at, :] = grads
        return total + jnp.sum(grads * grads, axis=0, keepdims=True)

    low = count.shape[1]
    total = lax.fori_loop(0, width // tile, one, jnp.zeros((1, low), f32))
    new = old_ref[...] + total / width
    new_ref[...] = new
    factor = learn_rate / (jnp.sqrt(new) + epsilon)
    step_ref[...] = step_ref[...] * factor


def steps_of(grad, count, old):
    width, bags = grad.shape
    highs, _, low = count.shape
    return pl.pallas_call(
        step_body,
        grid=(highs,),
        in_specs=[
            pl.BlockSpec((width, bags), lambda h: (0, 0)),
            pl.BlockSpec((1, bags, low), lambda h: (h, 0, 0)),
            pl.BlockSpec((1, low), lambda h: (0, h)),
        ],
        out_specs=[
            pl.BlockSpec((width, low), lambda h: (0, h)),
            pl.BlockSpec((1, low), lambda h: (0, h)),
        ],
        out_shape=(
            jax.ShapeDtypeStruct((width, highs * low), f32),
            jax.ShapeDtypeStruct((1, highs * low), f32),
        ),
        scratch_shapes=[pltpu.VMEM((width, bags), bf16), pltpu.VMEM((width, bags), bf16)],
        compiler_params=params(20),
        cost_estimate=pl.CostEstimate(flops=int(8e9), bytes_accessed=10 << 20, transcendentals=0),
        name="steps_of",
    )(grad, count, old)


def place_body(share, dest_ref, old_ref, step_ref, tgt_ref, after_ref, *refs):
    out_refs, (high_ref, low_ref, hold_ref, sems) = refs[:-4], refs[-4:]
    slices, narrow, n = old_ref.shape
    tgt = tgt_ref[...]

    def cut(f, carry):
        step = step_ref[pl.ds(pl.multiple_of((f * SHARES + share) * narrow, narrow), narrow), :]
        at = pl.ds(pl.multiple_of(f * narrow, narrow), narrow)
        high_ref[at, :], low_ref[at, :] = split(old_ref[f] - step)
        return carry

    lax.fori_loop(0, slices, cut, 0)
    slot = lax.broadcasted_iota(i32, (CAP, n), 0)
    copies = []
    for i, out_ref in enumerate(out_refs):
        here = jnp.where(slot == tgt - dest_ref[i] * CAP, 1.0, 0.0).astype(bf16)
        total = lax.dot_general(high_ref[...], here, NT, preferred_element_type=f32)
        total = total + lax.dot_general(low_ref[...], here, NT, preferred_element_type=f32)
        hold_ref[i] = total
        copies.append(pltpu.make_async_copy(hold_ref.at[i], out_ref, sems.at[i]))
        copies[-1].start()
    for copy in copies:
        copy.wait()


def place(share, dests, old, step, tgt, after):
    count = dests.shape[0]
    rows = old.shape[0] * old.shape[1]
    half = pltpu.VMEM((rows, old.shape[2]), bf16)
    return pl.pallas_call(
        functools.partial(place_body, share),
        in_specs=[SMEM, VMEM, VMEM, VMEM, ANY],
        out_specs=[HBM] * count,
        out_shape=(jax.ShapeDtypeStruct((rows, CAP), f32),) * count,
        scratch_shapes=[
            half,
            half,
            pltpu.VMEM((count, rows, CAP), f32),
            pltpu.SemaphoreType.DMA((count,)),
        ],
        compiler_params=params(12),
        cost_estimate=pl.CostEstimate(flops=int(2e9), bytes_accessed=6 << 20, transcendentals=0),
        name="place",
    )(dests, old, step, tgt, after)


def join_body(shares, at_ref, *refs):
    count = len(shares)
    parts, (out_ref, hold_ref, in_sems, out_sems) = refs[:count], refs[-4:]
    cap = hold_ref.shape[3]
    loads, stores = [], []
    for i, share in enumerate(shares):
        loads.append(pltpu.make_async_copy(parts[i], hold_ref.at[i], in_sems.at[i]))
        to = out_ref.at[:, share, :, pl.ds(pl.multiple_of(at_ref[i] * cap, cap), cap)]
        stores.append(pltpu.make_async_copy(hold_ref.at[i], to, out_sems.at[i]))
    for load in loads:
        load.start()
    for load, store in zip(loads, stores):
        load.wait()
        store.start()
    for store in stores:
        store.wait()


def join(shares, at, parts, whole, total, slices):
    count = len(parts)
    rows, cap = parts[0].shape
    narrow = rows // slices
    parts = [part.reshape(slices, narrow, cap) for part in parts]
    kept = () if whole is None else (whole,)
    return pl.pallas_call(
        functools.partial(join_body, shares),
        in_specs=[SMEM] + [HBM] * (count + len(kept)),
        out_specs=HBM,
        out_shape=jax.ShapeDtypeStruct((slices, SHARES, narrow, total * cap), f32),
        scratch_shapes=[
            pltpu.VMEM((count, slices, narrow, cap), f32),
            pltpu.SemaphoreType.DMA((count,)),
            pltpu.SemaphoreType.DMA((count,)),
        ],
        input_output_aliases={1 + count: 0} if kept else {},
        compiler_params=params(4),
        cost_estimate=pl.CostEstimate(flops=0, bytes_accessed=count << 19, transcendentals=0),
        name="join",
    )(jnp.stack(at), *parts, *kept)


def exchange(olds, step, tgt):
    count = lax.axis_size("row")
    chips, cores = count // 2, 2
    me = lax.axis_index("row")
    slices = olds[0].shape[0]

    def toward(dy, dc, of):
        y, core = of // cores, of % cores
        return (y + dy) % chips * cores + (core + dc) % cores

    def send(part, dy, dc):
        if (dy, dc) == (0, 0):
            return part
        return lax.ppermute(part, "row", [(s, toward(dy, dc, s)) for s in range(count)])

    near = [(1, 0), (chips - 1, 0), (1, 1), (chips - 1, 1)]
    far = [(dy, dc) for dy in range(2, chips - 1) for dc in range(2)]
    own = [(0, 1), (0, 0)]
    shifts = near + far + own
    dests = jnp.stack([toward(dy, dc, me) for dy, dc in shifts])
    got, made = {}, [tgt]
    for h, old in enumerate(olds):
        made = place(h, dests, old, step, tgt, made[0])
        for part, shift in zip(made, shifts):
            got[h, shift] = send(part, *shift)
    groups = []
    for h in range(SHARES):
        last = h == SHARES - 1
        groups.append([(h, shift) for shift in near + (own if last else [])])
        groups.append([(h, shift) for shift in far + ([] if last else own)])
    whole = None
    for group in groups:
        at = [toward(chips - dy, cores - dc, me) for _, (dy, dc) in group]
        whole = join(tuple(h for h, _ in group), at, [got[key] for key in group], whole, count, slices)
    return whole.reshape(-1, count * CAP)


def local(table, accum, grad_pooled, bag_of, slots, dirty_rows, owner):
    width_slice, bags = grad_pooled.shape
    col_count = lax.axis_size("col")
    col = lax.axis_index("col")
    n = dirty_rows.shape[1] // col_count
    grad = lax.all_gather(grad_pooled, "col", axis=0, tiled=True)
    tgt, accum_old = plan(col, dirty_rows, owner.T, accum, col_count)
    count = pair_counts(bag_of, slots, col, bags, n)
    picked = gather_rows(table, dirty_rows, col_count, count)
    step, accum_new = steps_of(grad, count, accum_old)
    later, step = lax.optimization_barrier((tuple(picked[1:]), step))
    olds = [lax.all_to_all(part, "col", 0, 0, tiled=True) for part in (picked[0], *later)]
    owned = exchange(olds, step, tgt)
    return owned, accum_new[0]


def solution(mesh):
    return jax.shard_map(
        local,
        mesh=mesh,
        in_specs=(
            P("col", "row"),
            P("row"),
            P("col", "row"),
            P("row", None),
            P("row", None),
            P("row", None),
            P("row", None),
        ),
        out_specs=(P(None, ("row", "col")), P(("row", "col"))),
        check_vma=False,
    )
```

time: 176 us -> 156 us (0.89)
  blocking collectives: 54.4 us -> 0 us
  starting transfers between devices: 7.88 us -> 34 us
  local copies, waits for them, and re-layouts: 7.55 us -> 19.4 us
  Pallas kernels: 72.9 us -> 69 us
  other arithmetic: 2.93 us -> 0.23 us
  waiting for transfers between devices: 15.5 us -> 17.5 us
    all_to_all x1 -> x0, blocking collectives: 54.4 us -> none  [local(): owned = join(lax.all_to_all(placed, 'row', 0, 0, tiled=True))]
    ppermute x0 -> x14, starting transfers between devices: none -> 21.1 us  [send(): lax.ppermute(part, 'row', [(s, toward(dy, dc, s)) for s in range(count)])]
    ppermute x0 -> x14, waiting for transfers between devices: none -> 14.3 us  [send(): lax.ppermute(part, 'row', [(s, toward(dy, dc, s)) for s in range(count)])]
    unnamed x16 -> x48, local copies, waits for them, and re-layouts: 6.5 us -> 19.2 us
    all_gather x1, waiting for transfers between devices: 14.8 us -> 2.53 us  [local(): grad = lax.all_gather(grad_pooled, 'col', axis=0, tiled=True)]
    all_to_all x1 -> x2, starting transfers between devices: 7.84 us -> 12.8 us  [local(): lax.all_to_all(part, 'col', 0, 0, tiled=True)]
    pallas_call x4 -> x8, Pallas kernels: 50.7 us -> 47.4 us  [the longest x1 28.8 us: gather_rows(): pl.pallas_call(gather_body, in_specs=[SMEM, VMEM, VMEM, ANY], out_specs=[...]
    unnamed x2 -> x0, other arithmetic: 2.82 us -> none
  transfers between devices with their start and end apart: 2 -> 17, of which waited for: 1 -> 6; matrix products, arithmetic and copies ran while one was open for 3% -> 0% of each run, Pallas kernels for 33% -> 44%
where the time goes in v3:
time: 156 us; the launch traced here: 154 us
  Pallas kernels  69 us (44%)
  starting transfers between devices  34 us (22%)
  local copies, waits for them, and re-layouts  19.4 us (12%)
  waiting for transfers between devices  17.5 us (11%)
  between operations  14.2 us (9%)
    pallas_call x1, Pallas kernels, gather_rows(): pl.pallas_call(gather_body, in_specs=[SMEM, VMEM, VMEM, ANY], out_specs=[...  28.8 us
    ppermute x14, starting transfers between devices, send(): lax.ppermute(part, 'row', [(s, toward(dy, dc, s)) for s in range(count)])  21.1 us
    unnamed x48, local copies, waits for them, and re-layouts  19.2 us
    ppermute x14, waiting for transfers between devices, send(): lax.ppermute(part, 'row', [(s, toward(dy, dc, s)) for s in range(count)])  14.3 us
    pallas_call x1, Pallas kernels, pair_counts(): pl.pallas_call(counts_body, out_shape=jax.ShapeDtypeStruct((span // LOW,...  13.9 us
    all_to_all x2, starting transfers between devices, local(): lax.all_to_all(part, 'col', 0, 0, tiled=True)  12.8 us
    pallas_call x2, Pallas kernels, place(): pl.pallas_call(functools.partial(place_body, share), in_specs=[SMEM, VMEM...  10.5 us
    pallas_call x1, Pallas kernels, steps_of(): pl.pallas_call(step_body, grid=(highs,), in_specs=[pl.BlockSpec((width, b...  7.76 us
  transfers between devices with their start and end apart: 17, of which 6 were waited for; matrix products, arithmetic and copies ran while one was open for 0% of the time, Pallas kernels for 44%

profile of v3, /device:TPU:7, one launch (start us, length us, event | category | flops | bytes accessed | tf_op | source)
XLA Modules:
  0.0 154.4 jit_solution(12098890273941016365)
XLA Ops:
  9.7 13.9 %pair_counts.1.after_ref.count_ref = bf16[4,2048,256]{2,1,0:T(8,128)(2,1)S(1)} custom-call(s32[1]{0:T(128)} %bitcast.9.block_ref.col_ref, s32[1,32768]{1,0:T(1,128)S(1)} %copy-done.19, s32[1,32768]{1,0:T(1,128)S(1)} %copy-done.19, s32[1,32768]{1,0:T(1,128)S(1)} %copy-done.20), custom_call_target="tpu_custom_call" | custom-call | flops 8000000000 | bytes 5242880 | tf_op jit(solution)/shard_map/pair_counts/pallas_call | solution.py:137
  23.6 28.8 %gather_rows.1 = (f32[16,16,1024]{2,1,0:T(8,128)}, f32[16,16,1024]{2,1,0:T(8,128)}) custom-call(s32[1,16384]{1,0:T(1,128)S(1)} %copy-done.3, s32[1,16384]{1,0:T(1,128)S(1)} %copy-done.3, f32[32,65536]{1,0:T(8,128)S(1)} %copy-done, bf16[4,2048,256]{2,1,0:T(8,128)(2,1)S(1)} %pair_counts.1.after_ref.count_ref), custom_call_target="tpu_custom_call" | custom-call | flops 1000000000 | bytes 10485760 | tf_op jit(solution)/shard_map/gather_rows/pallas_call | solution.py:195
  52.5 7.7 %all-to-all-start.1 = ((f32[16,16,1024]{2,1,0:T(8,128)}), f32[16,16,1024]{2,1,0:T(8,128)S(1)}, u32[]{:S(2)}, u32[]{:S(2)}) async-start(f32[16,16,1024]{2,1,0:T(8,128)} %get-tuple-element.32), calls=%async_computation.1 | async-start | bytes 2097152 | tf_op jit(solution)/shard_map/all_to_all | solution.py:401
  61.7 2.5 %all-gather.2.cloned.1.call-done.grad_ref = f32[512,2048]{1,0:T(8,128)} async-done(((f32[32,2048]{1,0:T(8,128)}), f32[512,2048]{1,0:T(8,128)}) %all-gather.2.cloned.1.call-update) | async-done | bytes 4194320 | tf_op jit(solution)/shard_map/all_gather | solution.py:395
  64.2 2.2 %copy-done.2 = bf16[4,2048,256]{2,1,0:T(8,128)(2,1)S(1)} copy-done((bf16[4,2048,256]{2,1,0:T(8,128)(2,1)S(1)}, bf16[4,2048,256]{2,1,0:T(8,128)(2,1)}, u32[]{:S(2)}) %copy-start.2) | copy-done | bytes 4194328
  66.4 2.2 %copy-done.12 = f32[512,2048]{1,0:T(8,128)S(1)} copy-done((f32[512,2048]{1,0:T(8,128)S(1)}, f32[512,2048]{1,0:T(8,128)}, u32[]{:S(2)}) %copy-start.12) | copy-done | bytes 4194328
  68.6 7.8 %steps_of.1 = (f32[512,1024]{1,0:T(8,128)S(1)}, f32[1,1024]{1,0:T(1,128)}) custom-call(f32[512,2048]{1,0:T(8,128)S(1)} %copy-done.12, bf16[4,2048,256]{2,1,0:T(8,128)(2,1)S(1)} %copy-done.2, f32[1,1024]{1,0:T(1,128)S(1)} %get-tuple-element.27.old_ref), custom_call_target="tpu_custom_call" | custom-call | flops 8000000000 | bytes 10485760 | tf_op jit(solution)/shard_map/steps_of/pallas_call | solution.py:243
  77.7 5.1 %all-to-all-start = ((f32[16,16,1024]{2,1,0:T(8,128)}), f32[16,16,1024]{2,1,0:T(8,128)S(1)}, u32[]{:S(2)}, u32[]{:S(2)}) async-start(f32[16,16,1024]{2,1,0:T(8,128)} %get-tuple-element.29), calls=%async_computation | async-start | bytes 2097152 | tf_op jit(solution)/shard_map/all_to_all | solution.py:401
  84.5 4.5 %place.2 = (f32[256,256]{1,0:T(8,128)S(1)}, f32[256,256]{1,0:T(8,128)}, f32[256,256]{1,0:T(8,128)}, f32[256,256]{1,0:T(8,128)}, f32[256,256]{1,0:T(8,128)S(1)}, ...) custom-call(s32[8]{0:T(128)S(1)} %stack.75.dest_ref, f32[16,16,1024]{2,1,0:T(8,128)S(1)} %all-to-all-done.1.old_ref, ...), custom_call_target="tpu_custom_call" | custom-call | flops 2000000000 | bytes 6291456 | tf_op jit(solution)/shard_map/place/pallas_call | solution.py:295
  89.0 2.8 %collective-permute-start.7 = (f32[256,256]{1,0:T(8,128)S(1)}, f32[256,256]{1,0:T(8,128)S(1)}, u32[]{:S(2)}, u32[]{:S(2)}) collective-permute-start(f32[256,256]{1,0:T(8,128)S(1)} %get-tuple-element.42), channel_id=1, source_target_pairs={{0,64},{16,80},{32,96},{48,112},{64,0},{80,16},{96,32},{112,48},{1... | collective-permute-start | bytes 786440 | tf_op jit(solution)/shard_map/ppermute | solution.py:366
  91.8 1.6 %collective-permute-start.8 = (f32[256,256]{1,0:T(8,128)}, f32[256,256]{1,0:T(8,128)S(1)}, u32[]{:S(2)}, u32[]{:S(2)}) collective-permute-start(f32[256,256]{1,0:T(8,128)} %get-tuple-element.43), channel_id=1, source_target_pairs={{0,80},{16,64},{32,112},{48,96},{64,16},{80,0},{96,48},{112,32},{1... | collective-permute-start | bytes 786440 | tf_op jit(solution)/shard_map/ppermute | solution.py:366
  93.5 2.5 %collective-permute-start.11 = (f32[256,256]{1,0:T(8,128)}, f32[256,256]{1,0:T(8,128)S(1)}, u32[]{:S(2)}, u32[]{:S(2)}) collective-permute-start(f32[256,256]{1,0:T(8,128)} %get-tuple-element.46), channel_id=1, source_target_pairs={{0,96},{16,112},{32,0},{48,16},{64,32},{80,48},{96,64},{112,80},{1... | collective-permute-start | bytes 786440 | tf_op jit(solution)/shard_map/ppermute | solution.py:366
  97.2 6.4 %collective-permute-start.13 = (f32[256,256]{1,0:T(8,128)}, f32[256,256]{1,0:T(8,128)S(1)}, u32[]{:S(2)}, u32[]{:S(2)}) collective-permute-start(f32[256,256]{1,0:T(8,128)} %get-tuple-element.48), channel_id=1, source_target_pairs={{0,112},{16,96},{32,16},{48,0},{64,48},{80,32},{96,80},{112,64},{1... | collective-permute-start | bytes 786440 | tf_op jit(solution)/shard_map/ppermute | solution.py:366
  105.1 5.9 %place.3 = (f32[256,256]{1,0:T(8,128)}, f32[256,256]{1,0:T(8,128)}, f32[256,256]{1,0:T(8,128)S(1)}, f32[256,256]{1,0:T(8,128)S(1)}, f32[256,256]{1,0:T(8,128)S(1...) custom-call(s32[8]{0:T(128)S(1)} %stack.75.dest_ref, ...), custom_call_target="tpu_custom_call" | custom-call | flops 2000000000 | bytes 6291456 | tf_op jit(solution)/shard_map/place/pallas_call | solution.py:295
  114.8 2.5 %collective-permute-start.3 = (f32[256,256]{1,0:T(8,128)}, f32[256,256]{1,0:T(8,128)S(1)}, u32[]{:S(2)}, u32[]{:S(2)}) collective-permute-start(f32[256,256]{1,0:T(8,128)} %get-tuple-element.37), channel_id=1, source_target_pairs={{0,96},{16,112},{32,0},{48,16},{64,32},{80,48},{96,64},{112,80},{1... | collective-permute-start | bytes 786440 | tf_op jit(solution)/shard_map/ppermute | solution.py:366
  119.9 1.7 %collective-permute-start.1 = (f32[256,256]{1,0:T(8,128)}, f32[256,256]{1,0:T(8,128)S(1)}, u32[]{:S(2)}, u32[]{:S(2)}) collective-permute-start(f32[256,256]{1,0:T(8,128)} %copy-done.13), channel_id=1, source_target_pairs={{0,80},{16,64},{32,112},{48,96},{64,16},{80,0},{96,48},{112,32},{1... | collective-permute-start | bytes 786440 | tf_op jit(solution)/shard_map/ppermute | solution.py:366
  121.6 2.8 %collective-permute-done.10 = f32[256,256]{1,0:T(8,128)S(1)} collective-permute-done((f32[256,256]{1,0:T(8,128)}, f32[256,256]{1,0:T(8,128)S(1)}, u32[]{:S(2)}, u32[]{:S(2)}) %collective-permute-start.10) | collective-permute-done | bytes 262176 | tf_op jit(solution)/shard_map/ppermute | solution.py:366
  125.1 2.2 %collective-permute-done.2 = f32[256,256]{1,0:T(8,128)S(1)} collective-permute-done((f32[256,256]{1,0:T(8,128)}, f32[256,256]{1,0:T(8,128)S(1)}, u32[]{:S(2)}, u32[]{:S(2)}) %collective-permute-start.2) | collective-permute-done | bytes 262176 | tf_op jit(solution)/shard_map/ppermute | solution.py:366
  127.3 2.3 %collective-permute-start.5 = (f32[256,256]{1,0:T(8,128)}, f32[256,256]{1,0:T(8,128)S(1)}, u32[]{:S(2)}, u32[]{:S(2)}) collective-permute-start(f32[256,256]{1,0:T(8,128)} %copy-done.16), channel_id=1, source_target_pairs={{0,112},{16,96},{32,16},{48,0},{64,48},{80,32},{96,80},{112,64},{1... | collective-permute-start | bytes 786440 | tf_op jit(solution)/shard_map/ppermute | solution.py:366
  129.6 5.3 %collective-permute-done.3 = f32[256,256]{1,0:T(8,128)S(1)} collective-permute-done((f32[256,256]{1,0:T(8,128)}, f32[256,256]{1,0:T(8,128)S(1)}, u32[]{:S(2)}, u32[]{:S(2)}) %collective-permute-start.3) | collective-permute-done | bytes 262176 | tf_op jit(solution)/shard_map/ppermute | solution.py:366
  138.1 1.7 %join.4.refs_4_ = f32[16,2,16,2048]{3,2,1,0:T(8,128)} custom-call(s32[4]{0:T(128)S(1)} %pad_add_fusion.2.at_ref, f32[16,16,256]{2,1,0:T(8,128)S(1)} %bitcast.50, f32[16,16,256]{2,1,0:T(8,128)S(1)} %bitcast.47, f32[16,16,256]{2,1,0:T(8,128)S(1)} %bitcast.48, f32[16,16,256]{2,1,0:T(8,128)S(1)} %bitcast.49), custom_call_target="tpu_custom_call" | custom-call | bytes 2097152 | tf_op jit(solution)/shard_map/join/pallas_call | solution.py:336
  139.7 1.7 %join.5.refs_6_ = f32[16,2,16,2048]{3,2,1,0:T(8,128)} custom-call(s32[4]{0:T(128)S(1)} %pad_add_fusion.1.at_ref, f32[16,16,256]{2,1,0:T(8,128)S(1)} %bitcast.35, f32[16,16,256]{2,1,0:T(8,128)S(1)} %bitcast.36, f32[16,16,256]{2,1,0:T(8,128)S(1)} %bitcast.37, f32[16,16,256]{2,1,0:T(8,128)S(1)} %bitcast.34, ...), custom_call_target="tpu_custom_call", output_to_operand_aliasing={{}: (5, {})} | custom-call | bytes 2097152 | tf_op jit(solution)/shard_map/join/pallas_call | solution.py:336
  141.4 2.8 %collective-permute-done.4 = f32[256,256]{1,0:T(8,128)S(1)} collective-permute-done((f32[256,256]{1,0:T(8,128)}, f32[256,256]{1,0:T(8,128)S(1)}, u32[]{:S(2)}, u32[]{:S(2)}) %collective-permute-start.4) | collective-permute-done | bytes 262176 | tf_op jit(solution)/shard_map/ppermute | solution.py:366
  144.2 1.9 %join.6.refs_2_ = f32[16,2,16,2048]{3,2,1,0:T(8,128)} custom-call(s32[6]{0:T(128)S(1)} %stack.80.at_ref, f32[16,16,256]{2,1,0:T(8,128)S(1)} %bitcast.39, f32[16,16,256]{2,1,0:T(8,128)S(1)} %bitcast.40, f32[16,16,256]{2,1,0:T(8,128)S(1)} %bitcast.43, f32[16,16,256]{2,1,0:T(8,128)S(1)} %bitcast.44, ...), custom_call_target="tpu_custom_call", output_to_operand_aliasing={{}: (7, {})} | custom-call | bytes 3145728 | tf_op jit(solution)/shard_map/join/pallas_call | solution.py:336
  (74 shorter events, 21.4 us)
Async XLA Ops:
  7.2 57.0 %all-gather.2.cloned.1.call-start = ((), (), s32[]{:S(2)}) async-start(), calls=%async_computation.2 | async-start | bytes 4456448 | tf_op jit(solution)/shard_map/all_gather | solution.py:395
  9.7 13.9 %copy-start = (f32[32,65536]{1,0:T(8,128)S(1)}, f32[32,65536]{1,0:T(8,128)}, u32[]{:S(2)}) copy-start(f32[32,65536]{1,0:T(8,128)} %table_ref.1) | copy-start | bytes 25165828
  9.7 13.9 %copy-start.3 = (s32[1,16384]{1,0:T(1,128)S(1)}, s32[1,16384]{1,0:T(1,128)}, u32[]{:S(2)}) copy-start(s32[1,16384]{1,0:T(1,128)} %row_ref.3) | copy-start | bytes 196612
  23.6 28.9 %copy-start.1 = (bf16[4,2048,256]{2,1,0:T(8,128)(2,1)}, bf16[4,2048,256]{2,1,0:T(8,128)(2,1)S(1)}, u32[]{:S(2)}) copy-start(bf16[4,2048,256]{2,1,0:T(8,128)(2,1)S(1)} %pair_counts.1.after_ref.count_ref) | copy-start | bytes 12582916
  23.6 36.6 %copy-start.4 = (f32[65536]{0:T(1024)S(1)}, f32[65536]{0:T(1024)}, u32[]{:S(2)}) copy-start(f32[65536]{0:T(1024)} %param.8) | copy-start | bytes 786436
  23.6 36.6 %copy-start.11 = (s32[16384,1]{0,1:T(1,128)S(1)}, s32[16384,1]{0,1:T(1,128)}, u32[]{:S(2)}) copy-start(s32[16384,1]{0,1:T(1,128)} %param.13) | copy-start | bytes 196612
  52.5 25.2 %all-to-all-start.1 = ((f32[16,16,1024]{2,1,0:T(8,128)}), f32[16,16,1024]{2,1,0:T(8,128)S(1)}, u32[]{:S(2)}, u32[]{:S(2)}) async-start(f32[16,16,1024]{2,1,0:T(8,128)} %get-tuple-element.32), calls=%async_computation.1 | async-start | bytes 2097152 | tf_op jit(solution)/shard_map/all_to_all | solution.py:401
  64.2 2.2 %copy-start.2 = (bf16[4,2048,256]{2,1,0:T(8,128)(2,1)S(1)}, bf16[4,2048,256]{2,1,0:T(8,128)(2,1)}, u32[]{:S(2)}) copy-start(bf16[4,2048,256]{2,1,0:T(8,128)(2,1)} %copy-done.1) | copy-start | bytes 12582916
  77.7 25.9 %all-to-all-start = ((f32[16,16,1024]{2,1,0:T(8,128)}), f32[16,16,1024]{2,1,0:T(8,128)S(1)}, u32[]{:S(2)}, u32[]{:S(2)}) async-start(f32[16,16,1024]{2,1,0:T(8,128)} %get-tuple-element.29), calls=%async_computation | async-start | bytes 2097152 | tf_op jit(solution)/shard_map/all_to_all | solution.py:401
  89.0 22.1 %copy-start.18 = (f32[256,256]{1,0:T(8,128)}, f32[256,256]{1,0:T(8,128)S(1)}, u32[]{:S(2)}) copy-start(f32[256,256]{1,0:T(8,128)S(1)} %get-tuple-element.33.after_ref) | copy-start | bytes 786436
  89.0 8.1 %collective-permute-start.7 = (f32[256,256]{1,0:T(8,128)S(1)}, f32[256,256]{1,0:T(8,128)S(1)}, u32[]{:S(2)}, u32[]{:S(2)}) collective-permute-start(f32[256,256]{1,0:T(8,128)S(1)} %get-tuple-element.42), channel_id=1, source_target_pairs={{0,64},{16,80},{32,96},{48,112},{64,0},{80,16},{96,32},{112,48},{1... | collective-permute-start | bytes 786440 | tf_op jit(solution)/shard_map/ppermute | solution.py:366
  91.8 22.8 %collective-permute-start.8 = (f32[256,256]{1,0:T(8,128)}, f32[256,256]{1,0:T(8,128)S(1)}, u32[]{:S(2)}, u32[]{:S(2)}) collective-permute-start(f32[256,256]{1,0:T(8,128)} %get-tuple-element.43), channel_id=1, source_target_pairs={{0,80},{16,64},{32,112},{48,96},{64,16},{80,0},{96,48},{112,32},{1... | collective-permute-start | bytes 786440 | tf_op jit(solution)/shard_map/ppermute | solution.py:366
  93.5 21.1 %collective-permute-start.9 = (f32[256,256]{1,0:T(8,128)}, f32[256,256]{1,0:T(8,128)S(1)}, u32[]{:S(2)}, u32[]{:S(2)}) collective-permute-start(f32[256,256]{1,0:T(8,128)} %get-tuple-element.44), channel_id=1, source_target_pairs={{0,16},{16,0},{32,48},{48,32},{64,80},{80,64},{96,112},{112,96},{1... | collective-permute-start | bytes 786440 | tf_op jit(solution)/shard_map/ppermute | solution.py:366
  93.5 21.4 %collective-permute-start.11 = (f32[256,256]{1,0:T(8,128)}, f32[256,256]{1,0:T(8,128)S(1)}, u32[]{:S(2)}, u32[]{:S(2)}) collective-permute-start(f32[256,256]{1,0:T(8,128)} %get-tuple-element.46), channel_id=1, source_target_pairs={{0,96},{16,112},{32,0},{48,16},{64,32},{80,48},{96,64},{112,80},{1... | collective-permute-start | bytes 786440 | tf_op jit(solution)/shard_map/ppermute | solution.py:366
  95.9 21.4 %collective-permute-start.12 = (f32[256,256]{1,0:T(8,128)}, f32[256,256]{1,0:T(8,128)S(1)}, u32[]{:S(2)}, u32[]{:S(2)}) collective-permute-start(f32[256,256]{1,0:T(8,128)} %get-tuple-element.47), channel_id=1, source_target_pairs={{0,48},{16,32},{32,80},{48,64},{64,112},{80,96},{96,16},{112,0},{1... | collective-permute-start | bytes 786440 | tf_op jit(solution)/shard_map/ppermute | solution.py:366
  97.2 22.1 %collective-permute-start.13 = (f32[256,256]{1,0:T(8,128)}, f32[256,256]{1,0:T(8,128)S(1)}, u32[]{:S(2)}, u32[]{:S(2)}) collective-permute-start(f32[256,256]{1,0:T(8,128)} %get-tuple-element.48), channel_id=1, source_target_pairs={{0,112},{16,96},{32,16},{48,0},{64,48},{80,32},{96,80},{112,64},{1... | collective-permute-start | bytes 786440 | tf_op jit(solution)/shard_map/ppermute | solution.py:366
  114.6 9.8 %collective-permute-start.10 = (f32[256,256]{1,0:T(8,128)}, f32[256,256]{1,0:T(8,128)S(1)}, u32[]{:S(2)}, u32[]{:S(2)}) collective-permute-start(f32[256,256]{1,0:T(8,128)} %copy-done.18), channel_id=1, source_target_pairs={{0,32},{16,48},{32,64},{48,80},{64,96},{80,112},{96,0},{112,16},{1... | collective-permute-start | bytes 786440 | tf_op jit(solution)/shard_map/ppermute | solution.py:366
  114.6 12.7 %collective-permute-start.2 = (f32[256,256]{1,0:T(8,128)}, f32[256,256]{1,0:T(8,128)S(1)}, u32[]{:S(2)}, u32[]{:S(2)}) collective-permute-start(f32[256,256]{1,0:T(8,128)} %get-tuple-element.36), channel_id=1, source_target_pairs={{0,32},{16,48},{32,64},{48,80},{64,96},{80,112},{96,0},{112,16},{1... | collective-permute-start | bytes 786440 | tf_op jit(solution)/shard_map/ppermute | solution.py:366
  114.8 20.1 %collective-permute-start.3 = (f32[256,256]{1,0:T(8,128)}, f32[256,256]{1,0:T(8,128)S(1)}, u32[]{:S(2)}, u32[]{:S(2)}) collective-permute-start(f32[256,256]{1,0:T(8,128)} %get-tuple-element.37), channel_id=1, source_target_pairs={{0,96},{16,112},{32,0},{48,16},{64,32},{80,48},{96,64},{112,80},{1... | collective-permute-start | bytes 786440 | tf_op jit(solution)/shard_map/ppermute | solution.py:366
  118.1 28.0 %collective-permute-start = (f32[256,256]{1,0:T(8,128)}, f32[256,256]{1,0:T(8,128)S(1)}, u32[]{:S(2)}, u32[]{:S(2)}) collective-permute-start(f32[256,256]{1,0:T(8,128)} %copy-done.14), channel_id=1, source_target_pairs={{0,64},{16,80},{32,96},{48,112},{64,0},{80,16},{96,32},{112,48},{1... | collective-permute-start | bytes 786440 | tf_op jit(solution)/shard_map/ppermute | solution.py:366
  119.9 26.2 %collective-permute-start.1 = (f32[256,256]{1,0:T(8,128)}, f32[256,256]{1,0:T(8,128)S(1)}, u32[]{:S(2)}, u32[]{:S(2)}) collective-permute-start(f32[256,256]{1,0:T(8,128)} %copy-done.13), channel_id=1, source_target_pairs={{0,80},{16,64},{32,112},{48,96},{64,16},{80,0},{96,48},{112,32},{1... | collective-permute-start | bytes 786440 | tf_op jit(solution)/shard_map/ppermute | solution.py:366
  125.1 19.0 %collective-permute-start.4 = (f32[256,256]{1,0:T(8,128)}, f32[256,256]{1,0:T(8,128)S(1)}, u32[]{:S(2)}, u32[]{:S(2)}) collective-permute-start(f32[256,256]{1,0:T(8,128)} %copy-done.17), channel_id=1, source_target_pairs={{0,48},{16,32},{32,80},{48,64},{64,112},{80,96},{96,16},{112,0},{1... | collective-permute-start | bytes 786440 | tf_op jit(solution)/shard_map/ppermute | solution.py:366
  127.3 16.9 %collective-permute-start.5 = (f32[256,256]{1,0:T(8,128)}, f32[256,256]{1,0:T(8,128)S(1)}, u32[]{:S(2)}, u32[]{:S(2)}) collective-permute-start(f32[256,256]{1,0:T(8,128)} %copy-done.16), channel_id=1, source_target_pairs={{0,112},{16,96},{32,16},{48,0},{64,48},{80,32},{96,80},{112,64},{1... | collective-permute-start | bytes 786440 | tf_op jit(solution)/shard_map/ppermute | solution.py:366
  134.9 9.3 %collective-permute-start.6 = (f32[256,256]{1,0:T(8,128)}, f32[256,256]{1,0:T(8,128)S(1)}, u32[]{:S(2)}, u32[]{:S(2)}) collective-permute-start(f32[256,256]{1,0:T(8,128)} %copy-done.15), channel_id=1, source_target_pairs={{0,16},{16,0},{32,48},{48,32},{64,80},{80,64},{96,112},{112,96},{1... | collective-permute-start | bytes 786440 | tf_op jit(solution)/shard_map/ppermute | solution.py:366
  (17 other events, 17.0 us)
Sparse Core Ops, SparseCore 0:
  10.1 54.0 all-gather.1

commit v4 on v3

--- a/solution.py
+++ b/solution.py
@@ -16,6 +16,8 @@
 BAGS = 64
 PAIRS = 5
 LOW = 256
+WHOLE = 60
+JOIN = 4
 SHARES = 2
 
 f32, bf16, i32 = jnp.float32, jnp.bfloat16, jnp.int32
@@ -207,116 +209,155 @@
     )(rows, rows, table, after)
 
 
-def step_body(grad_ref, count_ref, old_ref, step_ref, new_ref, high_ref, low_ref):
-    width = grad_ref.shape[0]
-    tile = 256
-
-    @pl.when(pl.program_id(0) == 0)
-    def _():
-        def cut(i, carry):
-            at = pl.ds(pl.multiple_of(i * 32, 32), 32)
-            high_ref[at, :], low_ref[at, :] = split(grad_ref[at, :])
+def step_body(grad_ref, count_ref, old_ref, step_ref, new_ref, *scratch):
+    wide_ref, both_ref, hold_ref, out_ref, grad_sems, count_sems, out_sems = scratch
+    width, bags = grad_ref.shape
+    highs, _, low = count_ref.shape
+    cuts = grad_sems.shape[0]
+    deep = width // cuts
+    assert both_ref.shape == (cuts, 2 * deep, bags)
+    grads = [
+        pltpu.make_async_copy(
+            grad_ref.at[i * deep : (i + 1) * deep, :],
+            wide_ref.at[i * deep : (i + 1) * deep, :],
+            grad_sems.at[i],
+        )
+        for i in range(cuts)
+    ]
+    counts = [
+        pltpu.make_async_copy(count_ref.at[h], hold_ref.at[h], count_sems.at[h])
+        for h in range(highs)
+    ]
+    outs = [
+        pltpu.make_async_copy(
+            out_ref.at[h], step_ref.at[:, h * low : (h + 1) * low], out_sems.at[h]
+        )
+        for h in range(highs)
+    ]
+    for copy in (*grads, counts[0]):
+        copy.start()
+    for i in range(cuts):
+        grads[i].wait()
+        if i == cuts - 1:
+            for copy in counts[1:]:
+                copy.start()
+
+        def cut(j, carry):
+            high, low = split(wide_ref[pl.ds(pl.multiple_of(i * deep + j * 32, 32), 32), :])
+            both_ref[i, pl.ds(pl.multiple_of(j * 32, 32), 32), :] = high
+            both_ref[i, pl.ds(pl.multiple_of(deep + j * 32, 32), 32), :] = low
             return carry
 
-        lax.fori_loop(0, width // 32, cut, 0)
-
-    count = count_ref[0]
-
-    def one(i, total):
-        at = pl.ds(pl.multiple_of(i * tile, tile), tile)
-        grads = lax.dot_general(high_ref[at, :], count, NN, preferred_element_type=f32)
-        grads = grads + lax.dot_general(low_ref[at, :], count, NN, preferred_element_type=f32)
-        step_ref[at, :] = grads
-        return total + jnp.sum(grads * grads, axis=0, keepdims=True)
-
-    low = count.shape[1]
-    total = lax.fori_loop(0, width // tile, one, jnp.zeros((1, low), f32))
-    new = old_ref[...] + total / width
-    new_ref[...] = new
-    factor = learn_rate / (jnp.sqrt(new) + epsilon)
-    step_ref[...] = step_ref[...] * factor
+        lax.fori_loop(0, deep // 32, cut, 0)
+
+    for h in range(highs):
+        counts[h].wait()
+
+        def one(i, total):
+            got = lax.dot_general(both_ref[i], hold_ref[h], NN, preferred_element_type=f32)
+            got = got[:deep] + got[deep:]
+            out_ref[h, pl.ds(pl.multiple_of(i * deep, deep), deep), :] = got
+            return total + jnp.sum(got * got, axis=0, keepdims=True)
+
+        total = lax.fori_loop(0, cuts, one, jnp.zeros((1, low), f32))
+        here = slice(h * low, (h + 1) * low)
+        new = old_ref[:, here] + total / width
+        new_ref[:, here] = new
+        out_ref[h] = out_ref[h] * (learn_rate / (jnp.sqrt(new) + epsilon))
+        outs[h].start()
+    for copy in outs:
+        copy.wait()
 
 
 def steps_of(grad, count, old):
     width, bags = grad.shape
     highs, _, low = count.shape
+    cuts = 2
     return pl.pallas_call(
         step_body,
-        grid=(highs,),
-        in_specs=[
-            pl.BlockSpec((width, bags), lambda h: (0, 0)),
-            pl.BlockSpec((1, bags, low), lambda h: (h, 0, 0)),
-            pl.BlockSpec((1, low), lambda h: (0, h)),
-        ],
-        out_specs=[
-            pl.BlockSpec((width, low), lambda h: (0, h)),
-            pl.BlockSpec((1, low), lambda h: (0, h)),
-        ],
+        in_specs=[HBM, HBM, VMEM],
+        out_specs=[HBM, VMEM],
         out_shape=(
             jax.ShapeDtypeStruct((width, highs * low), f32),
             jax.ShapeDtypeStruct((1, highs * low), f32),
         ),
-        scratch_shapes=[pltpu.VMEM((width, bags), bf16), pltpu.VMEM((width, bags), bf16)],
-        compiler_params=params(20),
+        scratch_shapes=[
+            pltpu.VMEM((width, bags), f32),
+            pltpu.VMEM((cuts, 2 * width // cuts, bags), bf16),
+            pltpu.VMEM(count.shape, bf16),
+            pltpu.VMEM((highs, width, low), f32),
+            pltpu.SemaphoreType.DMA((cuts,)),
+            pltpu.SemaphoreType.DMA((highs,)),
+            pltpu.SemaphoreType.DMA((highs,)),
+        ],
+        compiler_params=params(WHOLE),
         cost_estimate=pl.CostEstimate(flops=int(8e9), bytes_accessed=10 << 20, transcendentals=0),
         name="steps_of",
     )(grad, count, old)
 
 
-def place_body(share, dest_ref, old_ref, step_ref, tgt_ref, after_ref, *refs):
-    out_refs, (high_ref, low_ref, hold_ref, sems) = refs[:-4], refs[-4:]
+def place_body(share, towards, me_ref, old_ref, step_ref, tgt_ref, after_ref, *refs):
+    out_refs, scratch = refs[:-6], refs[-6:]
+    old_hold, step_hold, both_ref, hold_ref, loads, sems = scratch
     slices, narrow, n = old_ref.shape
+    rows = slices * narrow
     tgt = tgt_ref[...]
+    old_copy = pltpu.make_async_copy(old_ref, old_hold, loads.at[0])
+    step_copy = pltpu.make_async_copy(step_ref.at[:, share], step_hold, loads.at[1])
+    old_copy.start()
+    step_copy.start()
+    old_copy.wait()
+    step_copy.wait()
 
     def cut(f, carry):
-        step = step_ref[pl.ds(pl.multiple_of((f * SHARES + share) * narrow, narrow), narrow), :]
-        at = pl.ds(pl.multiple_of(f * narrow, narrow), narrow)
-        high_ref[at, :], low_ref[at, :] = split(old_ref[f] - step)
+        high, low = split(old_hold[f] - step_hold[f])
+        both_ref[pl.ds(pl.multiple_of(f * narrow, narrow), narrow), :] = high
+        both_ref[pl.ds(pl.multiple_of(rows + f * narrow, narrow), narrow), :] = low
         return carry
 
     lax.fori_loop(0, slices, cut, 0)
     slot = lax.broadcasted_iota(i32, (CAP, n), 0)
     copies = []
     for i, out_ref in enumerate(out_refs):
-        here = jnp.where(slot == tgt - dest_ref[i] * CAP, 1.0, 0.0).astype(bf16)
-        total = lax.dot_general(high_ref[...], here, NT, preferred_element_type=f32)
-        total = total + lax.dot_general(low_ref[...], here, NT, preferred_element_type=f32)
-        hold_ref[i] = total
+        here = jnp.where(slot == tgt - towards[i](me_ref[0]) * CAP, 1.0, 0.0).astype(bf16)
+        total = lax.dot_general(both_ref[...], here, NT, preferred_element_type=f32)
+        hold_ref[i] = total[:rows] + total[rows:]
         copies.append(pltpu.make_async_copy(hold_ref.at[i], out_ref, sems.at[i]))
         copies[-1].start()
     for copy in copies:
         copy.wait()
 
 
-def place(share, dests, old, step, tgt, after):
-    count = dests.shape[0]
+def place(share, towards, me, old, step, tgt, after):
+    count = len(towards)
     rows = old.shape[0] * old.shape[1]
-    half = pltpu.VMEM((rows, old.shape[2]), bf16)
-    return pl.pallas_call(
-        functools.partial(place_body, share),
-        in_specs=[SMEM, VMEM, VMEM, VMEM, ANY],
+    return pl.pallas_call(
+        functools.partial(place_body, share, towards),
+        in_specs=[SMEM, HBM, HBM, VMEM, ANY],
         out_specs=[HBM] * count,
         out_shape=(jax.ShapeDtypeStruct((rows, CAP), f32),) * count,
         scratch_shapes=[
-            half,
-            half,
+            pltpu.VMEM(old.shape, f32),
+            pltpu.VMEM(old.shape, f32),
+            pltpu.VMEM((2 * rows, old.shape[2]), bf16),
             pltpu.VMEM((count, rows, CAP), f32),
+            pltpu.SemaphoreType.DMA((2,)),
             pltpu.SemaphoreType.DMA((count,)),
         ],
-        compiler_params=params(12),
+        compiler_params=params(WHOLE),
         cost_estimate=pl.CostEstimate(flops=int(2e9), bytes_accessed=6 << 20, transcendentals=0),
         name="place",
-    )(dests, old, step, tgt, after)
-
-
-def join_body(shares, at_ref, *refs):
+    )(me, old, step.reshape(old.shape[0], SHARES, *old.shape[1:]), tgt, after)
+
+
+def join_body(shares, me_ref, *refs):
     count = len(shares)
     parts, (out_ref, hold_ref, in_sems, out_sems) = refs[:count], refs[-4:]
     cap = hold_ref.shape[3]
     loads, stores = [], []
-    for i, share in enumerate(shares):
+    for i, (share, source) in enumerate(shares):
         loads.append(pltpu.make_async_copy(parts[i], hold_ref.at[i], in_sems.at[i]))
-        to = out_ref.at[:, share, :, pl.ds(pl.multiple_of(at_ref[i] * cap, cap), cap)]
+        to = out_ref.at[:, share, :, pl.ds(pl.multiple_of(source(me_ref[0]) * cap, cap), cap)]
         stores.append(pltpu.make_async_copy(hold_ref.at[i], to, out_sems.at[i]))
     for load in loads:
         load.start()
@@ -327,7 +368,7 @@
         store.wait()
 
 
-def join(shares, at, parts, whole, total, slices):
+def join(shares, me, parts, whole, total, slices):
     count = len(parts)
     rows, cap = parts[0].shape
     narrow = rows // slices
@@ -335,7 +376,7 @@
     kept = () if whole is None else (whole,)
     return pl.pallas_call(
         functools.partial(join_body, shares),
-        in_specs=[SMEM] + [HBM] * (count + len(kept)),
+        in_specs=[SMEM] + [ANY] * count + [HBM] * len(kept),
         out_specs=HBM,
         out_shape=jax.ShapeDtypeStruct((slices, SHARES, narrow, total * cap), f32),
         scratch_shapes=[
@@ -344,17 +385,17 @@
             pltpu.SemaphoreType.DMA((count,)),
         ],
         input_output_aliases={1 + count: 0} if kept else {},
-        compiler_params=params(4),
+        compiler_params=params(JOIN),
         cost_estimate=pl.CostEstimate(flops=0, bytes_accessed=count << 19, transcendentals=0),
         name="join",
-    )(jnp.stack(at), *parts, *kept)
-
-
-def exchange(olds, step, tgt):
+    )(me, *parts, *kept)
+
+
+def exchange(picked, step, tgt):
     count = lax.axis_size("row")
     chips, cores = count // 2, 2
-    me = lax.axis_index("row")
-    slices = olds[0].shape[0]
+    me = lax.axis_index("row").astype(i32)[None]
+    slices = lax.axis_size("col")
 
     def toward(dy, dc, of):
         y, core = of // cores, of % cores
@@ -368,22 +409,30 @@
     near = [(1, 0), (chips - 1, 0), (1, 1), (chips - 1, 1)]
     far = [(dy, dc) for dy in range(2, chips - 1) for dc in range(2)]
     own = [(0, 1), (0, 0)]
-    shifts = near + far + own
-    dests = jnp.stack([toward(dy, dc, me) for dy, dc in shifts])
+    shifts = far + near + own
+    towards = [functools.partial(toward, dy, dc) for dy, dc in shifts]
+    sources = [functools.partial(toward, chips - dy, cores - dc) for dy, dc in shifts]
+    first, *later = picked
+    later, step = lax.optimization_barrier((later, step))
     got, made = {}, [tgt]
-    for h, old in enumerate(olds):
-        made = place(h, dests, old, step, tgt, made[0])
-        for part, shift in zip(made, shifts):
-            got[h, shift] = send(part, *shift)
+    for h, part in enumerate([first, *later]):
+        old = lax.all_to_all(part, "col", 0, 0, tiled=True)
+        made = list(place(h, towards, me, old, step, tgt, made[0]))
+        for i, part in enumerate(made):
+            got[h, i] = send(part, *shifts[i])
     groups = []
     for h in range(SHARES):
-        last = h == SHARES - 1
-        groups.append([(h, shift) for shift in near + (own if last else [])])
-        groups.append([(h, shift) for shift in far + ([] if last else own)])
+        first = [(h, i) for i in range(len(far))]
+        later = [(h, len(far) + i) for i in range(len(near))]
+        mine = [(h, len(near) + len(far) + i) for i in range(len(own))]
+        if h == SHARES - 1:
+            groups += [first + mine, later[:2], later[2:]]
+        else:
+            groups += [first + mine, later]
     whole = None
     for group in groups:
-        at = [toward(chips - dy, cores - dc, me) for _, (dy, dc) in group]
-        whole = join(tuple(h for h, _ in group), at, [got[key] for key in group], whole, count, slices)
+        shares = tuple((h, sources[i]) for h, i in group)
+        whole = join(shares, me, [got[key] for key in group], whole, count, slices)
     return whole.reshape(-1, count * CAP)
 
 
@@ -397,9 +446,7 @@
     count = pair_counts(bag_of, slots, col, bags, n)
     picked = gather_rows(table, dirty_rows, col_count, count)
     step, accum_new = steps_of(grad, count, accum_old)
-    later, step = lax.optimization_barrier((tuple(picked[1:]), step))
-    olds = [lax.all_to_all(part, "col", 0, 0, tiled=True) for part in (picked[0], *later)]
-    owned = exchange(olds, step, tgt)
+    owned = exchange(picked, step, tgt)
     return owned, accum_new[0]
 
 

time: 156 us -> 145 us (0.929)
  local copies, waits for them, and re-layouts: 19.4 us -> 3.99 us
  starting transfers between devices: 34 us -> 37 us
  Pallas kernels: 69 us -> 71.5 us
    unnamed x48 -> x28, local copies, waits for them, and re-layouts: 19.2 us -> 3.99 us
    ppermute x14, starting transfers between devices: 21.1 us -> 24 us  [send(): lax.ppermute(part, 'row', [(s, toward(dy, dc, s)) for s in range(count)])]
    pallas_call x7 -> x8, Pallas kernels: 24.8 us -> 27.4 us  [the longest x2 11.6 us: place(): pl.pallas_call(functools.partial(place_body, share, towards), in_specs=[S...]
  transfers between devices with their start and end apart: 17 -> 17, of which waited for: 6 -> 6; matrix products, arithmetic and copies ran while one was open for 0% -> 0% of each run, Pallas kernels for 44% -> 49%
where the time goes in v4:
time: 145 us; the launch traced here: 144 us
  Pallas kernels  71.5 us (49%)
  starting transfers between devices  37 us (26%)
  waiting for transfers between devices  17.4 us (12%)
  between operations  14.3 us (10%)
  local copies, waits for them, and re-layouts  3.99 us (3%)
    pallas_call x1, Pallas kernels, gather_rows(): pl.pallas_call(gather_body, in_specs=[SMEM, VMEM, VMEM, ANY], out_specs=[...  28.8 us
    ppermute x14, starting transfers between devices, send(): lax.ppermute(part, 'row', [(s, toward(dy, dc, s)) for s in range(count)])  24 us
    ppermute x14, waiting for transfers between devices, send(): lax.ppermute(part, 'row', [(s, toward(dy, dc, s)) for s in range(count)])  15.3 us
    pallas_call x1, Pallas kernels, pair_counts(): pl.pallas_call(counts_body, out_shape=jax.ShapeDtypeStruct((span // LOW,...  13.9 us
    all_to_all x2, starting transfers between devices, exchange(): old = lax.all_to_all(part, 'col', 0, 0, tiled=True)  13 us
    pallas_call x2, Pallas kernels, place(): pl.pallas_call(functools.partial(place_body, share, towards), in_specs=[S...  11.6 us
    pallas_call x1, Pallas kernels, steps_of(): pl.pallas_call(step_body, in_specs=[HBM, HBM, VMEM], out_specs=[HBM, VMEM...  10.7 us
    pallas_call x5, Pallas kernels, join(): pl.pallas_call(functools.partial(join_body, shares), in_specs=[SMEM] + [A...  5.09 us
  transfers between devices with their start and end apart: 17, of which 6 were waited for; matrix products, arithmetic and copies ran while one was open for 0% of the time, Pallas kernels for 49%

profile of v4, /device:TPU:7, one launch (start us, length us, event | category | flops | bytes accessed | tf_op | source)
XLA Modules:
  0.0 144.2 jit_solution(16656420983454604966)
XLA Ops:
  9.7 13.9 %pair_counts.1.after_ref.count_ref = bf16[4,2048,256]{2,1,0:T(8,128)(2,1)S(1)} custom-call(s32[1]{0:T(128)} %bitcast.1.block_ref.col_ref, s32[1,32768]{1,0:T(1,128)S(1)} %copy-done.7, s32[1,32768]{1,0:T(1,128)S(1)} %copy-done.7, s32[1,32768]{1,0:T(1,128)S(1)} %copy-done.8), custom_call_target="tpu_custom_call" | custom-call | flops 8000000000 | bytes 5242880 | tf_op jit(solution)/shard_map/pair_counts/pallas_call | solution.py:139
  23.6 28.8 %gather_rows.1 = (f32[16,16,1024]{2,1,0:T(8,128)}, f32[16,16,1024]{2,1,0:T(8,128)}) custom-call(s32[1,16384]{1,0:T(1,128)S(1)} %copy-done.2, s32[1,16384]{1,0:T(1,128)S(1)} %copy-done.2, f32[32,65536]{1,0:T(8,128)S(1)} %copy-done, bf16[4,2048,256]{2,1,0:T(8,128)(2,1)S(1)} %pair_counts.1.after_ref.count_ref), custom_call_target="tpu_custom_call" | custom-call | flops 1000000000 | bytes 10485760 | tf_op jit(solution)/shard_map/gather_rows/pallas_call | solution.py:197
  52.4 7.7 %all-to-all-start.1 = ((f32[16,16,1024]{2,1,0:T(8,128)}), f32[16,16,1024]{2,1,0:T(8,128)S(1)}, u32[]{:S(2)}, u32[]{:S(2)}) async-start(f32[16,16,1024]{2,1,0:T(8,128)} %get-tuple-element.32), calls=%async_computation.1 | async-start | bytes 2097152 | tf_op jit(solution)/shard_map/all_to_all | solution.py:419
  60.2 1.4 %plan.1 = (s32[1,1024]{1,0:T(1,128)S(1)}, f32[1,1024]{1,0:T(1,128)S(1)}) custom-call(s32[1]{0:T(128)} %bitcast.1.block_ref.col_ref, s32[1,16384]{1,0:T(1,128)S(1)} %copy-done.2, s32[1,16384]{1,0:T(1,128)S(1)} %bitcast.40, f32[512,128]{1,0:T(8,128)S(1)} %bitcast.35), custom_call_target="tpu_custom_call" | custom-call | tf_op jit(solution)/shard_map/plan/pallas_call | solution.py:68
  62.8 1.4 all-gather.2.cloned.1.call-done.grad_ref
  64.2 10.7 %steps_of.1 = (f32[512,1024]{1,0:T(8,128)}, f32[1,1024]{1,0:T(1,128)}) custom-call(f32[512,2048]{1,0:T(8,128)} %all-gather.2.cloned.1.call-done.grad_ref, bf16[4,2048,256]{2,1,0:T(8,128)(2,1)} %copy-done.1, f32[1,1024]{1,0:T(1,128)} %copy-done.10), custom_call_target="tpu_custom_call" | custom-call | flops 8000000000 | bytes 10485760 | tf_op jit(solution)/shard_map/steps_of/pallas_call | solution.py:276
  75.0 5.3 %all-to-all-start = ((f32[16,16,1024]{2,1,0:T(8,128)}), f32[16,16,1024]{2,1,0:T(8,128)S(1)}, u32[]{:S(2)}, u32[]{:S(2)}) async-start(f32[16,16,1024]{2,1,0:T(8,128)} %get-tuple-element.29), calls=%async_computation | async-start | bytes 2097152 | tf_op jit(solution)/shard_map/all_to_all | solution.py:419
  80.3 5.8 %place.2 = (f32[256,256]{1,0:T(8,128)}, f32[256,256]{1,0:T(8,128)}, f32[256,256]{1,0:T(8,128)}, f32[256,256]{1,0:T(8,128)}, f32[256,256]{1,0:T(8,128)}, /*index=...) custom-call(s32[1]{0:T(128)} %bitcast.me_ref, f32[16,16,1024]{2,1,0:T(8,128)} %copy-done.12, ...), custom_call_target="tpu_custom_call" | custom-call | flops 2000000000 | bytes 6291456 | tf_op jit(solution)/shard_map/place/pallas_call | solution.py:334
  86.1 1.4 collective-permute-start.7
  87.5 1.5 %collective-permute-start.8 = (f32[256,256]{1,0:T(8,128)}, f32[256,256]{1,0:T(8,128)S(1)}, u32[]{:S(2)}, u32[]{:S(2)}) collective-permute-start(f32[256,256]{1,0:T(8,128)} %get-tuple-element.43), channel_id=1, source_target_pairs={{0,96},{16,112},{32,0},{48,16},{64,32},{80,48},{96,64},{112,80},{1... | collective-permute-start | bytes 786440 | tf_op jit(solution)/shard_map/ppermute | solution.py:407
  89.0 2.8 %collective-permute-start.9 = (f32[256,256]{1,0:T(8,128)}, f32[256,256]{1,0:T(8,128)S(1)}, u32[]{:S(2)}, u32[]{:S(2)}) collective-permute-start(f32[256,256]{1,0:T(8,128)} %get-tuple-element.44), channel_id=1, source_target_pairs={{0,48},{16,32},{32,80},{48,64},{64,112},{80,96},{96,16},{112,0},{1... | collective-permute-start | bytes 786440 | tf_op jit(solution)/shard_map/ppermute | solution.py:407
  91.8 1.4 collective-permute-start.10
  93.3 1.9 %collective-permute-start.12 = (f32[256,256]{1,0:T(8,128)}, f32[256,256]{1,0:T(8,128)S(1)}, u32[]{:S(2)}, u32[]{:S(2)}) collective-permute-start(f32[256,256]{1,0:T(8,128)} %get-tuple-element.46), channel_id=1, source_target_pairs={{0,80},{16,64},{32,112},{48,96},{64,16},{80,0},{96,48},{112,32},{1... | collective-permute-start | bytes 786440 | tf_op jit(solution)/shard_map/ppermute | solution.py:407
  95.2 1.3 collective-permute-start.13
  97.4 5.8 %place.3 = (f32[256,256]{1,0:T(8,128)}, f32[256,256]{1,0:T(8,128)}, f32[256,256]{1,0:T(8,128)}, f32[256,256]{1,0:T(8,128)}, f32[256,256]{1,0:T(8,128)}, /*index=...) custom-call(s32[1]{0:T(128)} %bitcast.me_ref, f32[16,16,1024]{2,1,0:T(8,128)} %copy-done.11, ...), custom_call_target="tpu_custom_call" | custom-call | flops 2000000000 | bytes 6291456 | tf_op jit(solution)/shard_map/place/pallas_call | solution.py:334
  103.3 3.0 %collective-permute-start.11 = (f32[256,256]{1,0:T(8,128)S(1)}, f32[256,256]{1,0:T(8,128)S(1)}, u32[]{:S(2)}, u32[]{:S(2)}) collective-permute-start(f32[256,256]{1,0:T(8,128)S(1)} %copy-done.13), channel_id=1, source_target_pairs={{0,64},{16,80},{32,96},{48,112},{64,0},{80,16},{96,32},{112,48},{1... | collective-permute-start | bytes 786440 | tf_op jit(solution)/shard_map/ppermute | solution.py:407
  106.3 3.6 %collective-permute-start.5 = (f32[256,256]{1,0:T(8,128)}, f32[256,256]{1,0:T(8,128)S(1)}, u32[]{:S(2)}, u32[]{:S(2)}) collective-permute-start(f32[256,256]{1,0:T(8,128)} %get-tuple-element.39), channel_id=1, source_target_pairs={{0,80},{16,64},{32,112},{48,96},{64,16},{80,0},{96,48},{112,32},{1... | collective-permute-start | bytes 786440 | tf_op jit(solution)/shard_map/ppermute | solution.py:407
  110.9 2.4 %collective-permute-done.11 = f32[256,256]{1,0:T(8,128)S(1)} collective-permute-done((f32[256,256]{1,0:T(8,128)S(1)}, f32[256,256]{1,0:T(8,128)S(1)}, u32[]{:S(2)}, u32[]{:S(2)}) %collective-permute-start.11) | collective-permute-done | bytes 262176 | tf_op jit(solution)/shard_map/ppermute | solution.py:407
  113.2 2.1 %collective-permute-start.3 = (f32[256,256]{1,0:T(8,128)}, f32[256,256]{1,0:T(8,128)S(1)}, u32[]{:S(2)}, u32[]{:S(2)}) collective-permute-start(f32[256,256]{1,0:T(8,128)} %get-tuple-element.37), channel_id=1, source_target_pairs={{0,96},{16,112},{32,0},{48,16},{64,32},{80,48},{96,64},{112,80},{1... | collective-permute-start | bytes 786440 | tf_op jit(solution)/shard_map/ppermute | solution.py:407
  115.3 3.6 %collective-permute-done.4 = f32[256,256]{1,0:T(8,128)S(1)} collective-permute-done((f32[256,256]{1,0:T(8,128)}, f32[256,256]{1,0:T(8,128)S(1)}, u32[]{:S(2)}, u32[]{:S(2)}) %collective-permute-start.4) | collective-permute-done | bytes 262176 | tf_op jit(solution)/shard_map/ppermute | solution.py:407
  118.9 3.1 %collective-permute-start = (f32[256,256]{1,0:T(8,128)}, f32[256,256]{1,0:T(8,128)S(1)}, u32[]{:S(2)}, u32[]{:S(2)}) collective-permute-start(f32[256,256]{1,0:T(8,128)} %get-tuple-element.34), channel_id=1, source_target_pairs={{0,48},{16,32},{32,80},{48,64},{64,112},{80,96},{96,16},{112,0},{1... | collective-permute-start | bytes 786440 | tf_op jit(solution)/shard_map/ppermute | solution.py:407
  121.9 4.0 %collective-permute-done.5 = f32[256,256]{1,0:T(8,128)S(1)} collective-permute-done((f32[256,256]{1,0:T(8,128)}, f32[256,256]{1,0:T(8,128)S(1)}, u32[]{:S(2)}, u32[]{:S(2)}) %collective-permute-start.5) | collective-permute-done | bytes 262176 | tf_op jit(solution)/shard_map/ppermute | solution.py:407
  129.2 1.1 join.7.refs_2_
  131.8 4.7 %collective-permute-done = f32[256,256]{1,0:T(8,128)S(1)} collective-permute-done((f32[256,256]{1,0:T(8,128)}, f32[256,256]{1,0:T(8,128)S(1)}, u32[]{:S(2)}, u32[]{:S(2)}) %collective-permute-start) | collective-permute-done | bytes 262176 | tf_op jit(solution)/shard_map/ppermute | solution.py:407
  (50 shorter events, 11.2 us)
Async XLA Ops:
  7.2 57.1 %all-gather.2.cloned.1.call-start = ((), (), s32[]{:S(2)}) async-start(), calls=%async_computation.2 | async-start | bytes 4456448 | tf_op jit(solution)/shard_map/all_gather | solution.py:444
  9.7 13.9 %copy-start = (f32[32,65536]{1,0:T(8,128)S(1)}, f32[32,65536]{1,0:T(8,128)}, u32[]{:S(2)}) copy-start(f32[32,65536]{1,0:T(8,128)} %table_ref.1) | copy-start | bytes 25165828
  9.7 13.9 %copy-start.2 = (s32[1,16384]{1,0:T(1,128)S(1)}, s32[1,16384]{1,0:T(1,128)}, u32[]{:S(2)}) copy-start(s32[1,16384]{1,0:T(1,128)} %row_ref.3) | copy-start | bytes 196612
  23.6 28.8 %copy-start.1 = (bf16[4,2048,256]{2,1,0:T(8,128)(2,1)}, bf16[4,2048,256]{2,1,0:T(8,128)(2,1)S(1)}, u32[]{:S(2)}) copy-start(bf16[4,2048,256]{2,1,0:T(8,128)(2,1)S(1)} %pair_counts.1.after_ref.count_ref) | copy-start | bytes 12582916
  23.6 36.5 %copy-start.4 = (f32[65536]{0:T(1024)S(1)}, f32[65536]{0:T(1024)}, u32[]{:S(2)}) copy-start(f32[65536]{0:T(1024)} %param.8) | copy-start | bytes 786436
  23.6 36.5 %copy-start.6 = (s32[16384,1]{0,1:T(1,128)S(1)}, s32[16384,1]{0,1:T(1,128)}, u32[]{:S(2)}) copy-start(s32[16384,1]{0,1:T(1,128)} %param.13) | copy-start | bytes 196612
  52.4 22.5 %all-to-all-start.1 = ((f32[16,16,1024]{2,1,0:T(8,128)}), f32[16,16,1024]{2,1,0:T(8,128)S(1)}, u32[]{:S(2)}, u32[]{:S(2)}) async-start(f32[16,16,1024]{2,1,0:T(8,128)} %get-tuple-element.32), calls=%async_computation.1 | async-start | bytes 2097152 | tf_op jit(solution)/shard_map/all_to_all | solution.py:419
  75.0 21.5 %all-to-all-start = ((f32[16,16,1024]{2,1,0:T(8,128)}), f32[16,16,1024]{2,1,0:T(8,128)S(1)}, u32[]{:S(2)}, u32[]{:S(2)}) async-start(f32[16,16,1024]{2,1,0:T(8,128)} %get-tuple-element.29), calls=%async_computation | async-start | bytes 2097152 | tf_op jit(solution)/shard_map/all_to_all | solution.py:419
  86.1 17.2 %copy-start.13 = (f32[256,256]{1,0:T(8,128)S(1)}, f32[256,256]{1,0:T(8,128)}, u32[]{:S(2)}) copy-start(f32[256,256]{1,0:T(8,128)} %get-tuple-element.33.after_ref) | copy-start | bytes 786436
  86.1 40.8 %copy-start.5 = (f32[256,256]{1,0:T(8,128)S(1)}, f32[256,256]{1,0:T(8,128)}, u32[]{:S(2)}) copy-start(f32[256,256]{1,0:T(8,128)} %get-tuple-element.48) | copy-start | bytes 786436
  86.1 9.0 %collective-permute-start.7 = (f32[256,256]{1,0:T(8,128)}, f32[256,256]{1,0:T(8,128)S(1)}, u32[]{:S(2)}, u32[]{:S(2)}) collective-permute-start(f32[256,256]{1,0:T(8,128)} %get-tuple-element.42), channel_id=1, source_target_pairs={{0,32},{16,48},{32,64},{48,80},{64,96},{80,112},{96,0},{112,16},{1... | collective-permute-start | bytes 786440 | tf_op jit(solution)/shard_map/ppermute | solution.py:407
  87.5 15.8 %collective-permute-start.8 = (f32[256,256]{1,0:T(8,128)}, f32[256,256]{1,0:T(8,128)S(1)}, u32[]{:S(2)}, u32[]{:S(2)}) collective-permute-start(f32[256,256]{1,0:T(8,128)} %get-tuple-element.43), channel_id=1, source_target_pairs={{0,96},{16,112},{32,0},{48,16},{64,32},{80,48},{96,64},{112,80},{1... | collective-permute-start | bytes 786440 | tf_op jit(solution)/shard_map/ppermute | solution.py:407
  89.0 17.2 %collective-permute-start.9 = (f32[256,256]{1,0:T(8,128)}, f32[256,256]{1,0:T(8,128)S(1)}, u32[]{:S(2)}, u32[]{:S(2)}) collective-permute-start(f32[256,256]{1,0:T(8,128)} %get-tuple-element.44), channel_id=1, source_target_pairs={{0,48},{16,32},{32,80},{48,64},{64,112},{80,96},{96,16},{112,0},{1... | collective-permute-start | bytes 786440 | tf_op jit(solution)/shard_map/ppermute | solution.py:407
  91.8 14.5 %collective-permute-start.10 = (f32[256,256]{1,0:T(8,128)}, f32[256,256]{1,0:T(8,128)S(1)}, u32[]{:S(2)}, u32[]{:S(2)}) collective-permute-start(f32[256,256]{1,0:T(8,128)} %get-tuple-element.45), channel_id=1, source_target_pairs={{0,112},{16,96},{32,16},{48,0},{64,48},{80,32},{96,80},{112,64},{1... | collective-permute-start | bytes 786440 | tf_op jit(solution)/shard_map/ppermute | solution.py:407
  93.3 16.6 %collective-permute-start.12 = (f32[256,256]{1,0:T(8,128)}, f32[256,256]{1,0:T(8,128)S(1)}, u32[]{:S(2)}, u32[]{:S(2)}) collective-permute-start(f32[256,256]{1,0:T(8,128)} %get-tuple-element.46), channel_id=1, source_target_pairs={{0,80},{16,64},{32,112},{48,96},{64,16},{80,0},{96,48},{112,32},{1... | collective-permute-start | bytes 786440 | tf_op jit(solution)/shard_map/ppermute | solution.py:407
  95.2 14.8 %collective-permute-start.13 = (f32[256,256]{1,0:T(8,128)}, f32[256,256]{1,0:T(8,128)S(1)}, u32[]{:S(2)}, u32[]{:S(2)}) collective-permute-start(f32[256,256]{1,0:T(8,128)} %get-tuple-element.47), channel_id=1, source_target_pairs={{0,16},{16,0},{32,48},{48,32},{64,80},{80,64},{96,112},{112,96},{1... | collective-permute-start | bytes 786440 | tf_op jit(solution)/shard_map/ppermute | solution.py:407
  103.3 10.0 %collective-permute-start.11 = (f32[256,256]{1,0:T(8,128)S(1)}, f32[256,256]{1,0:T(8,128)S(1)}, u32[]{:S(2)}, u32[]{:S(2)}) collective-permute-start(f32[256,256]{1,0:T(8,128)S(1)} %copy-done.13), channel_id=1, source_target_pairs={{0,64},{16,80},{32,96},{48,112},{64,0},{80,16},{96,32},{112,48},{1... | collective-permute-start | bytes 786440 | tf_op jit(solution)/shard_map/ppermute | solution.py:407
  106.2 12.6 %collective-permute-start.4 = (f32[256,256]{1,0:T(8,128)}, f32[256,256]{1,0:T(8,128)S(1)}, u32[]{:S(2)}, u32[]{:S(2)}) collective-permute-start(f32[256,256]{1,0:T(8,128)} %get-tuple-element.38), channel_id=1, source_target_pairs={{0,64},{16,80},{32,96},{48,112},{64,0},{80,16},{96,32},{112,48},{1... | collective-permute-start | bytes 786440 | tf_op jit(solution)/shard_map/ppermute | solution.py:407
  106.3 19.6 %collective-permute-start.5 = (f32[256,256]{1,0:T(8,128)}, f32[256,256]{1,0:T(8,128)S(1)}, u32[]{:S(2)}, u32[]{:S(2)}) collective-permute-start(f32[256,256]{1,0:T(8,128)} %get-tuple-element.39), channel_id=1, source_target_pairs={{0,80},{16,64},{32,112},{48,96},{64,16},{80,0},{96,48},{112,32},{1... | collective-permute-start | bytes 786440 | tf_op jit(solution)/shard_map/ppermute | solution.py:407
  109.9 19.2 %collective-permute-start.6 = (f32[256,256]{1,0:T(8,128)}, f32[256,256]{1,0:T(8,128)S(1)}, u32[]{:S(2)}, u32[]{:S(2)}) collective-permute-start(f32[256,256]{1,0:T(8,128)} %get-tuple-element.40), channel_id=1, source_target_pairs={{0,16},{16,0},{32,48},{48,32},{64,80},{80,64},{96,112},{112,96},{1... | collective-permute-start | bytes 786440 | tf_op jit(solution)/shard_map/ppermute | solution.py:407
  109.9 20.9 %collective-permute-start.2 = (f32[256,256]{1,0:T(8,128)}, f32[256,256]{1,0:T(8,128)S(1)}, u32[]{:S(2)}, u32[]{:S(2)}) collective-permute-start(f32[256,256]{1,0:T(8,128)} %get-tuple-element.36), channel_id=1, source_target_pairs={{0,32},{16,48},{32,64},{48,80},{64,96},{80,112},{96,0},{112,16},{1... | collective-permute-start | bytes 786440 | tf_op jit(solution)/shard_map/ppermute | solution.py:407
  113.2 17.7 %collective-permute-start.3 = (f32[256,256]{1,0:T(8,128)}, f32[256,256]{1,0:T(8,128)S(1)}, u32[]{:S(2)}, u32[]{:S(2)}) collective-permute-start(f32[256,256]{1,0:T(8,128)} %get-tuple-element.37), channel_id=1, source_target_pairs={{0,96},{16,112},{32,0},{48,16},{64,32},{80,48},{96,64},{112,80},{1... | collective-permute-start | bytes 786440 | tf_op jit(solution)/shard_map/ppermute | solution.py:407
  118.9 17.6 %collective-permute-start = (f32[256,256]{1,0:T(8,128)}, f32[256,256]{1,0:T(8,128)S(1)}, u32[]{:S(2)}, u32[]{:S(2)}) collective-permute-start(f32[256,256]{1,0:T(8,128)} %get-tuple-element.34), channel_id=1, source_target_pairs={{0,48},{16,32},{32,80},{48,64},{64,112},{80,96},{96,16},{112,0},{1... | collective-permute-start | bytes 786440 | tf_op jit(solution)/shard_map/ppermute | solution.py:407
  126.0 10.5 %collective-permute-start.1 = (f32[256,256]{1,0:T(8,128)}, f32[256,256]{1,0:T(8,128)S(1)}, u32[]{:S(2)}, u32[]{:S(2)}) collective-permute-start(f32[256,256]{1,0:T(8,128)} %get-tuple-element.35), channel_id=1, source_target_pairs={{0,112},{16,96},{32,16},{48,0},{64,48},{80,32},{96,80},{112,64},{1... | collective-permute-start | bytes 786440 | tf_op jit(solution)/shard_map/ppermute | solution.py:407
  (7 other events, 10.4 us)
Sparse Core Ops, SparseCore 0:
  10.1 54.0 all-gather.1

commit v5 on v4

--- a/solution.py
+++ b/solution.py
@@ -302,12 +302,19 @@
     slices, narrow, n = old_ref.shape
     rows = slices * narrow
     tgt = tgt_ref[...]
-    old_copy = pltpu.make_async_copy(old_ref, old_hold, loads.at[0])
-    step_copy = pltpu.make_async_copy(step_ref.at[:, share], step_hold, loads.at[1])
-    old_copy.start()
-    step_copy.start()
-    old_copy.wait()
-    step_copy.wait()
+    chunks = loads.shape[0]
+    deep = slices // chunks
+    waits = []
+    for i in range(chunks):
+        at = slice(i * deep, (i + 1) * deep)
+        waits.append(
+            (
+                pltpu.make_async_copy(old_ref.at[at], old_hold.at[at], loads.at[i, 0]),
+                pltpu.make_async_copy(step_ref.at[at, share], step_hold.at[at], loads.at[i, 1]),
+            )
+        )
+        for copy in waits[-1]:
+            copy.start()
 
     def cut(f, carry):
         high, low = split(old_hold[f] - step_hold[f])
@@ -315,7 +322,10 @@
         both_ref[pl.ds(pl.multiple_of(rows + f * narrow, narrow), narrow), :] = low
         return carry
 
-    lax.fori_loop(0, slices, cut, 0)
+    for i in range(chunks):
+        for copy in waits[i]:
+            copy.wait()
+        lax.fori_loop(i * deep, (i + 1) * deep, cut, 0, unroll=True)
     slot = lax.broadcasted_iota(i32, (CAP, n), 0)
     copies = []
     for i, out_ref in enumerate(out_refs):
@@ -341,7 +351,7 @@
             pltpu.VMEM(old.shape, f32),
             pltpu.VMEM((2 * rows, old.shape[2]), bf16),
             pltpu.VMEM((count, rows, CAP), f32),
-            pltpu.SemaphoreType.DMA((2,)),
+            pltpu.SemaphoreType.DMA((4, 2)),
             pltpu.SemaphoreType.DMA((count,)),
         ],
         compiler_params=params(WHOLE),

time: 145 us -> 148 us (1.021)
  starting transfers between devices: 37 us -> 48.5 us
  waiting for transfers between devices: 17.4 us -> 10.2 us
    ppermute x14, starting transfers between devices: 24 us -> 35.5 us  [send(): lax.ppermute(part, 'row', [(s, toward(dy, dc, s)) for s in range(count)])]
    ppermute x14, waiting for transfers between devices: 15.3 us -> 8.06 us  [send(): lax.ppermute(part, 'row', [(s, toward(dy, dc, s)) for s in range(count)])]
  transfers between devices with their start and end apart: 17 -> 17, of which waited for: 6 -> 4; matrix products, arithmetic and copies ran while one was open for 0% -> 0% of each run, Pallas kernels for 49% -> 47%
where the time goes in v5:
time: 148 us
  Pallas kernels  71 us (48%)
  starting transfers between devices  48.5 us (33%)
  between operations  14.3 us (10%)
  waiting for transfers between devices  10.2 us (7%)
  local copies, waits for them, and re-layouts  3.99 us (3%)
    ppermute x14, starting transfers between devices, send(): lax.ppermute(part, 'row', [(s, toward(dy, dc, s)) for s in range(count)])  35.5 us
    pallas_call x1, Pallas kernels, gather_rows(): pl.pallas_call(gather_body, in_specs=[SMEM, VMEM, VMEM, ANY], out_specs=[...  28.8 us
    pallas_call x1, Pallas kernels, pair_counts(): pl.pallas_call(counts_body, out_shape=jax.ShapeDtypeStruct((span // LOW,...  13.9 us
    all_to_all x2, starting transfers between devices, exchange(): old = lax.all_to_all(part, 'col', 0, 0, tiled=True)  13 us
    pallas_call x2, Pallas kernels, place(): pl.pallas_call(functools.partial(place_body, share, towards), in_specs=[S...  11.1 us
    pallas_call x1, Pallas kernels, steps_of(): pl.pallas_call(step_body, in_specs=[HBM, HBM, VMEM], out_specs=[HBM, VMEM...  10.7 us
    ppermute x14, waiting for transfers between devices, send(): lax.ppermute(part, 'row', [(s, toward(dy, dc, s)) for s in range(count)])  8.06 us
    pallas_call x5, Pallas kernels, join(): pl.pallas_call(functools.partial(join_body, shares), in_specs=[SMEM] + [A...  5.09 us
  transfers between devices with their start and end apart: 17, of which 4 were waited for; matrix products, arithmetic and copies ran while one was open for 0% of the time, Pallas kernels for 47%

profile of v5, /device:TPU:7, one launch (start us, length us, event | category | flops | bytes accessed | tf_op | source)
XLA Modules:
  0.0 147.9 jit_solution(11286124676617191803)
XLA Ops:
  9.7 13.9 %pair_counts.1.after_ref.count_ref = bf16[4,2048,256]{2,1,0:T(8,128)(2,1)S(1)} custom-call(s32[1]{0:T(128)} %bitcast.1.block_ref.col_ref, s32[1,32768]{1,0:T(1,128)S(1)} %copy-done.7, s32[1,32768]{1,0:T(1,128)S(1)} %copy-done.7, s32[1,32768]{1,0:T(1,128)S(1)} %copy-done.8), custom_call_target="tpu_custom_call" | custom-call | flops 8000000000 | bytes 5242880 | tf_op jit(solution)/shard_map/pair_counts/pallas_call | solution.py:139
  23.6 28.8 %gather_rows.1 = (f32[16,16,1024]{2,1,0:T(8,128)}, f32[16,16,1024]{2,1,0:T(8,128)}) custom-call(s32[1,16384]{1,0:T(1,128)S(1)} %copy-done.2, s32[1,16384]{1,0:T(1,128)S(1)} %copy-done.2, f32[32,65536]{1,0:T(8,128)S(1)} %copy-done, bf16[4,2048,256]{2,1,0:T(8,128)(2,1)S(1)} %pair_counts.1.after_ref.count_ref), custom_call_target="tpu_custom_call" | custom-call | flops 1000000000 | bytes 10485760 | tf_op jit(solution)/shard_map/gather_rows/pallas_call | solution.py:197
  52.4 7.7 %all-to-all-start.1 = ((f32[16,16,1024]{2,1,0:T(8,128)}), f32[16,16,1024]{2,1,0:T(8,128)S(1)}, u32[]{:S(2)}, u32[]{:S(2)}) async-start(f32[16,16,1024]{2,1,0:T(8,128)} %get-tuple-element.32), calls=%async_computation.1 | async-start | bytes 2097152 | tf_op jit(solution)/shard_map/all_to_all | solution.py:429
  60.2 1.4 plan.1
  62.8 1.4 all-gather.2.cloned.1.call-done.grad_ref
  64.2 10.7 %steps_of.1 = (f32[512,1024]{1,0:T(8,128)}, f32[1,1024]{1,0:T(1,128)}) custom-call(f32[512,2048]{1,0:T(8,128)} %all-gather.2.cloned.1.call-done.grad_ref, bf16[4,2048,256]{2,1,0:T(8,128)(2,1)} %copy-done.1, f32[1,1024]{1,0:T(1,128)} %copy-done.10), custom_call_target="tpu_custom_call" | custom-call | flops 8000000000 | bytes 10485760 | tf_op jit(solution)/shard_map/steps_of/pallas_call | solution.py:276
  75.0 5.3 %all-to-all-start = ((f32[16,16,1024]{2,1,0:T(8,128)}), f32[16,16,1024]{2,1,0:T(8,128)S(1)}, u32[]{:S(2)}, u32[]{:S(2)}) async-start(f32[16,16,1024]{2,1,0:T(8,128)} %get-tuple-element.29), calls=%async_computation | async-start | bytes 2097152 | tf_op jit(solution)/shard_map/all_to_all | solution.py:429
  80.3 5.6 %place.2 = (f32[256,256]{1,0:T(8,128)}, f32[256,256]{1,0:T(8,128)}, f32[256,256]{1,0:T(8,128)}, f32[256,256]{1,0:T(8,128)}, f32[256,256]{1,0:T(8,128)}, /*index=...) custom-call(s32[1]{0:T(128)} %bitcast.me_ref, f32[16,16,1024]{2,1,0:T(8,128)} %copy-done.12, ...), custom_call_target="tpu_custom_call" | custom-call | flops 2000000000 | bytes 6291456 | tf_op jit(solution)/shard_map/place/pallas_call | solution.py:344
  85.8 1.4 collective-permute-start.7
  87.2 1.5 %collective-permute-start.8 = (f32[256,256]{1,0:T(8,128)}, f32[256,256]{1,0:T(8,128)S(1)}, u32[]{:S(2)}, u32[]{:S(2)}) collective-permute-start(f32[256,256]{1,0:T(8,128)} %get-tuple-element.43), channel_id=1, source_target_pairs={{0,96},{16,112},{32,0},{48,16},{64,32},{80,48},{96,64},{112,80},{1... | collective-permute-start | bytes 786440 | tf_op jit(solution)/shard_map/ppermute | solution.py:417
  88.7 2.9 %collective-permute-start.9 = (f32[256,256]{1,0:T(8,128)}, f32[256,256]{1,0:T(8,128)S(1)}, u32[]{:S(2)}, u32[]{:S(2)}) collective-permute-start(f32[256,256]{1,0:T(8,128)} %get-tuple-element.44), channel_id=1, source_target_pairs={{0,48},{16,32},{32,80},{48,64},{64,112},{80,96},{96,16},{112,0},{1... | collective-permute-start | bytes 786440 | tf_op jit(solution)/shard_map/ppermute | solution.py:417
  91.6 1.4 collective-permute-start.10
  93.0 1.9 %collective-permute-start.12 = (f32[256,256]{1,0:T(8,128)}, f32[256,256]{1,0:T(8,128)S(1)}, u32[]{:S(2)}, u32[]{:S(2)}) collective-permute-start(f32[256,256]{1,0:T(8,128)} %get-tuple-element.46), channel_id=1, source_target_pairs={{0,80},{16,64},{32,112},{48,96},{64,16},{80,0},{96,48},{112,32},{1... | collective-permute-start | bytes 786440 | tf_op jit(solution)/shard_map/ppermute | solution.py:417
  94.9 1.3 collective-permute-start.13
  97.2 5.5 %place.3 = (f32[256,256]{1,0:T(8,128)}, f32[256,256]{1,0:T(8,128)}, f32[256,256]{1,0:T(8,128)}, f32[256,256]{1,0:T(8,128)}, f32[256,256]{1,0:T(8,128)}, /*index=...) custom-call(s32[1]{0:T(128)} %bitcast.me_ref, f32[16,16,1024]{2,1,0:T(8,128)} %copy-done.11, ...), custom_call_target="tpu_custom_call" | custom-call | flops 2000000000 | bytes 6291456 | tf_op jit(solution)/shard_map/place/pallas_call | solution.py:344
  102.7 3.0 %collective-permute-start.11 = (f32[256,256]{1,0:T(8,128)S(1)}, f32[256,256]{1,0:T(8,128)S(1)}, u32[]{:S(2)}, u32[]{:S(2)}) collective-permute-start(f32[256,256]{1,0:T(8,128)S(1)} %copy-done.13), channel_id=1, source_target_pairs={{0,64},{16,80},{32,96},{48,112},{64,0},{80,16},{96,32},{112,48},{1... | collective-permute-start | bytes 786440 | tf_op jit(solution)/shard_map/ppermute | solution.py:417
  105.9 3.8 %collective-permute-start.5 = (f32[256,256]{1,0:T(8,128)}, f32[256,256]{1,0:T(8,128)S(1)}, u32[]{:S(2)}, u32[]{:S(2)}) collective-permute-start(f32[256,256]{1,0:T(8,128)} %get-tuple-element.39), channel_id=1, source_target_pairs={{0,80},{16,64},{32,112},{48,96},{64,16},{80,0},{96,48},{112,32},{1... | collective-permute-start | bytes 786440 | tf_op jit(solution)/shard_map/ppermute | solution.py:417
  109.7 15.2 %collective-permute-start.2 = (f32[256,256]{1,0:T(8,128)}, f32[256,256]{1,0:T(8,128)S(1)}, u32[]{:S(2)}, u32[]{:S(2)}) collective-permute-start(f32[256,256]{1,0:T(8,128)} %get-tuple-element.36), channel_id=1, source_target_pairs={{0,32},{16,48},{32,64},{48,80},{64,96},{80,112},{96,0},{112,16},{1... | collective-permute-start | bytes 786440 | tf_op jit(solution)/shard_map/ppermute | solution.py:417
  124.9 2.0 %collective-permute-start = (f32[256,256]{1,0:T(8,128)}, f32[256,256]{1,0:T(8,128)S(1)}, u32[]{:S(2)}, u32[]{:S(2)}) collective-permute-start(f32[256,256]{1,0:T(8,128)} %get-tuple-element.34), channel_id=1, source_target_pairs={{0,48},{16,32},{32,80},{48,64},{64,112},{80,96},{96,16},{112,0},{1... | collective-permute-start | bytes 786440 | tf_op jit(solution)/shard_map/ppermute | solution.py:417
  129.0 1.1 join.6.refs_4_
  130.2 1.1 join.7.refs_2_
  131.3 2.6 %collective-permute-done.3 = f32[256,256]{1,0:T(8,128)S(1)} collective-permute-done((f32[256,256]{1,0:T(8,128)}, f32[256,256]{1,0:T(8,128)S(1)}, u32[]{:S(2)}, u32[]{:S(2)}) %collective-permute-start.3) | collective-permute-done | bytes 262176 | tf_op jit(solution)/shard_map/ppermute | solution.py:417
  134.8 1.6 %collective-permute-done = f32[256,256]{1,0:T(8,128)S(1)} collective-permute-done((f32[256,256]{1,0:T(8,128)}, f32[256,256]{1,0:T(8,128)S(1)}, u32[]{:S(2)}, u32[]{:S(2)}) %collective-permute-start) | collective-permute-done | bytes 262176 | tf_op jit(solution)/shard_map/ppermute | solution.py:417
  136.4 3.8 %collective-permute-done.1 = f32[256,256]{1,0:T(8,128)S(1)} collective-permute-done((f32[256,256]{1,0:T(8,128)}, f32[256,256]{1,0:T(8,128)S(1)}, u32[]{:S(2)}, u32[]{:S(2)}) %collective-permute-start.1) | collective-permute-done | bytes 262176 | tf_op jit(solution)/shard_map/ppermute | solution.py:417
  (50 shorter events, 8.7 us)
Async XLA Ops:
  7.2 57.0 %all-gather.2.cloned.1.call-start = ((), (), s32[]{:S(2)}) async-start(), calls=%async_computation.2 | async-start | bytes 4456448 | tf_op jit(solution)/shard_map/all_gather | solution.py:454
  9.7 13.9 %copy-start = (f32[32,65536]{1,0:T(8,128)S(1)}, f32[32,65536]{1,0:T(8,128)}, u32[]{:S(2)}) copy-start(f32[32,65536]{1,0:T(8,128)} %table_ref.1) | copy-start | bytes 25165828
  9.7 13.9 %copy-start.2 = (s32[1,16384]{1,0:T(1,128)S(1)}, s32[1,16384]{1,0:T(1,128)}, u32[]{:S(2)}) copy-start(s32[1,16384]{1,0:T(1,128)} %row_ref.3) | copy-start | bytes 196612
  23.6 28.8 %copy-start.1 = (bf16[4,2048,256]{2,1,0:T(8,128)(2,1)}, bf16[4,2048,256]{2,1,0:T(8,128)(2,1)S(1)}, u32[]{:S(2)}) copy-start(bf16[4,2048,256]{2,1,0:T(8,128)(2,1)S(1)} %pair_counts.1.after_ref.count_ref) | copy-start | bytes 12582916
  23.6 36.5 %copy-start.4 = (f32[65536]{0:T(1024)S(1)}, f32[65536]{0:T(1024)}, u32[]{:S(2)}) copy-start(f32[65536]{0:T(1024)} %param.8) | copy-start | bytes 786436
  23.6 36.5 %copy-start.6 = (s32[16384,1]{0,1:T(1,128)S(1)}, s32[16384,1]{0,1:T(1,128)}, u32[]{:S(2)}) copy-start(s32[16384,1]{0,1:T(1,128)} %param.13) | copy-start | bytes 196612
  52.4 22.5 %all-to-all-start.1 = ((f32[16,16,1024]{2,1,0:T(8,128)}), f32[16,16,1024]{2,1,0:T(8,128)S(1)}, u32[]{:S(2)}, u32[]{:S(2)}) async-start(f32[16,16,1024]{2,1,0:T(8,128)} %get-tuple-element.32), calls=%async_computation.1 | async-start | bytes 2097152 | tf_op jit(solution)/shard_map/all_to_all | solution.py:429
  75.0 21.2 %all-to-all-start = ((f32[16,16,1024]{2,1,0:T(8,128)}), f32[16,16,1024]{2,1,0:T(8,128)S(1)}, u32[]{:S(2)}, u32[]{:S(2)}) async-start(f32[16,16,1024]{2,1,0:T(8,128)} %get-tuple-element.29), calls=%async_computation | async-start | bytes 2097152 | tf_op jit(solution)/shard_map/all_to_all | solution.py:429
  85.8 16.9 %copy-start.13 = (f32[256,256]{1,0:T(8,128)S(1)}, f32[256,256]{1,0:T(8,128)}, u32[]{:S(2)}) copy-start(f32[256,256]{1,0:T(8,128)} %get-tuple-element.33.after_ref) | copy-start | bytes 786436
  85.8 42.1 %copy-start.5 = (f32[256,256]{1,0:T(8,128)S(1)}, f32[256,256]{1,0:T(8,128)}, u32[]{:S(2)}) copy-start(f32[256,256]{1,0:T(8,128)} %get-tuple-element.48) | copy-start | bytes 786436
  85.8 9.1 %collective-permute-start.7 = (f32[256,256]{1,0:T(8,128)}, f32[256,256]{1,0:T(8,128)S(1)}, u32[]{:S(2)}, u32[]{:S(2)}) collective-permute-start(f32[256,256]{1,0:T(8,128)} %get-tuple-element.42), channel_id=1, source_target_pairs={{0,32},{16,48},{32,64},{48,80},{64,96},{80,112},{96,0},{112,16},{1... | collective-permute-start | bytes 786440 | tf_op jit(solution)/shard_map/ppermute | solution.py:417
  87.2 15.5 %collective-permute-start.8 = (f32[256,256]{1,0:T(8,128)}, f32[256,256]{1,0:T(8,128)S(1)}, u32[]{:S(2)}, u32[]{:S(2)}) collective-permute-start(f32[256,256]{1,0:T(8,128)} %get-tuple-element.43), channel_id=1, source_target_pairs={{0,96},{16,112},{32,0},{48,16},{64,32},{80,48},{96,64},{112,80},{1... | collective-permute-start | bytes 786440 | tf_op jit(solution)/shard_map/ppermute | solution.py:417
  88.7 17.0 %collective-permute-start.9 = (f32[256,256]{1,0:T(8,128)}, f32[256,256]{1,0:T(8,128)S(1)}, u32[]{:S(2)}, u32[]{:S(2)}) collective-permute-start(f32[256,256]{1,0:T(8,128)} %get-tuple-element.44), channel_id=1, source_target_pairs={{0,48},{16,32},{32,80},{48,64},{64,112},{80,96},{96,16},{112,0},{1... | collective-permute-start | bytes 786440 | tf_op jit(solution)/shard_map/ppermute | solution.py:417
  91.6 14.3 %collective-permute-start.10 = (f32[256,256]{1,0:T(8,128)}, f32[256,256]{1,0:T(8,128)S(1)}, u32[]{:S(2)}, u32[]{:S(2)}) collective-permute-start(f32[256,256]{1,0:T(8,128)} %get-tuple-element.45), channel_id=1, source_target_pairs={{0,112},{16,96},{32,16},{48,0},{64,48},{80,32},{96,80},{112,64},{1... | collective-permute-start | bytes 786440 | tf_op jit(solution)/shard_map/ppermute | solution.py:417
  93.0 16.7 %collective-permute-start.12 = (f32[256,256]{1,0:T(8,128)}, f32[256,256]{1,0:T(8,128)S(1)}, u32[]{:S(2)}, u32[]{:S(2)}) collective-permute-start(f32[256,256]{1,0:T(8,128)} %get-tuple-element.46), channel_id=1, source_target_pairs={{0,80},{16,64},{32,112},{48,96},{64,16},{80,0},{96,48},{112,32},{1... | collective-permute-start | bytes 786440 | tf_op jit(solution)/shard_map/ppermute | solution.py:417
  94.9 14.8 %collective-permute-start.13 = (f32[256,256]{1,0:T(8,128)}, f32[256,256]{1,0:T(8,128)S(1)}, u32[]{:S(2)}, u32[]{:S(2)}) collective-permute-start(f32[256,256]{1,0:T(8,128)} %get-tuple-element.47), channel_id=1, source_target_pairs={{0,16},{16,0},{32,48},{48,32},{64,80},{80,64},{96,112},{112,96},{1... | collective-permute-start | bytes 786440 | tf_op jit(solution)/shard_map/ppermute | solution.py:417
  102.7 22.1 %collective-permute-start.11 = (f32[256,256]{1,0:T(8,128)S(1)}, f32[256,256]{1,0:T(8,128)S(1)}, u32[]{:S(2)}, u32[]{:S(2)}) collective-permute-start(f32[256,256]{1,0:T(8,128)S(1)} %copy-done.13), channel_id=1, source_target_pairs={{0,64},{16,80},{32,96},{48,112},{64,0},{80,16},{96,32},{112,48},{1... | collective-permute-start | bytes 786440 | tf_op jit(solution)/shard_map/ppermute | solution.py:417
  105.8 19.1 %collective-permute-start.4 = (f32[256,256]{1,0:T(8,128)}, f32[256,256]{1,0:T(8,128)S(1)}, u32[]{:S(2)}, u32[]{:S(2)}) collective-permute-start(f32[256,256]{1,0:T(8,128)} %get-tuple-element.38), channel_id=1, source_target_pairs={{0,64},{16,80},{32,96},{48,112},{64,0},{80,16},{96,32},{112,48},{1... | collective-permute-start | bytes 786440 | tf_op jit(solution)/shard_map/ppermute | solution.py:417
  105.9 21.0 %collective-permute-start.5 = (f32[256,256]{1,0:T(8,128)}, f32[256,256]{1,0:T(8,128)S(1)}, u32[]{:S(2)}, u32[]{:S(2)}) collective-permute-start(f32[256,256]{1,0:T(8,128)} %get-tuple-element.39), channel_id=1, source_target_pairs={{0,80},{16,64},{32,112},{48,96},{64,16},{80,0},{96,48},{112,32},{1... | collective-permute-start | bytes 786440 | tf_op jit(solution)/shard_map/ppermute | solution.py:417
  109.7 20.5 %collective-permute-start.6 = (f32[256,256]{1,0:T(8,128)}, f32[256,256]{1,0:T(8,128)S(1)}, u32[]{:S(2)}, u32[]{:S(2)}) collective-permute-start(f32[256,256]{1,0:T(8,128)} %get-tuple-element.40), channel_id=1, source_target_pairs={{0,16},{16,0},{32,48},{48,32},{64,80},{80,64},{96,112},{112,96},{1... | collective-permute-start | bytes 786440 | tf_op jit(solution)/shard_map/ppermute | solution.py:417
  109.7 21.6 %collective-permute-start.2 = (f32[256,256]{1,0:T(8,128)}, f32[256,256]{1,0:T(8,128)S(1)}, u32[]{:S(2)}, u32[]{:S(2)}) collective-permute-start(f32[256,256]{1,0:T(8,128)} %get-tuple-element.36), channel_id=1, source_target_pairs={{0,32},{16,48},{32,64},{48,80},{64,96},{80,112},{96,0},{112,16},{1... | collective-permute-start | bytes 786440 | tf_op jit(solution)/shard_map/ppermute | solution.py:417
  124.9 9.1 %collective-permute-start.3 = (f32[256,256]{1,0:T(8,128)}, f32[256,256]{1,0:T(8,128)S(1)}, u32[]{:S(2)}, u32[]{:S(2)}) collective-permute-start(f32[256,256]{1,0:T(8,128)} %get-tuple-element.37), channel_id=1, source_target_pairs={{0,96},{16,112},{32,0},{48,16},{64,32},{80,48},{96,64},{112,80},{1... | collective-permute-start | bytes 786440 | tf_op jit(solution)/shard_map/ppermute | solution.py:417
  124.9 11.6 %collective-permute-start = (f32[256,256]{1,0:T(8,128)}, f32[256,256]{1,0:T(8,128)S(1)}, u32[]{:S(2)}, u32[]{:S(2)}) collective-permute-start(f32[256,256]{1,0:T(8,128)} %get-tuple-element.34), channel_id=1, source_target_pairs={{0,48},{16,32},{32,80},{48,64},{64,112},{80,96},{96,16},{112,0},{1... | collective-permute-start | bytes 786440 | tf_op jit(solution)/shard_map/ppermute | solution.py:417
  126.8 13.4 %collective-permute-start.1 = (f32[256,256]{1,0:T(8,128)}, f32[256,256]{1,0:T(8,128)S(1)}, u32[]{:S(2)}, u32[]{:S(2)}) collective-permute-start(f32[256,256]{1,0:T(8,128)} %get-tuple-element.35), channel_id=1, source_target_pairs={{0,112},{16,96},{32,16},{48,0},{64,48},{80,32},{96,80},{112,64},{1... | collective-permute-start | bytes 786440 | tf_op jit(solution)/shard_map/ppermute | solution.py:417
  (7 other events, 10.4 us)
Sparse Core Ops, SparseCore 0:
  10.1 54.0 all-gather.1
